TPU v7x, 32 devices: a whole 2x2x4 slice. The times are simulated.
32 devices in a mesh: dp: 4 (over z), ctx: 8 (over y, x, core).
Axes of the slice: x: 2, y: 2, z: 4, core: 2. Of those that a mesh axis runs over, the one named last changes fastest.
Arguments:
- queries: bfloat16 [4, 1024, 2048], P('dp', 'ctx'), may hold values from -6 to 6
- keys: bfloat16 [4, 1024, 2048], P('dp', 'ctx'), may hold values from -6 to 6
- values: bfloat16 [4, 1024, 2048], P('dp', 'ctx'), may hold values from -6 to 6
- grad_output: bfloat16 [4, 1024, 2048], P('dp', 'ctx'), may hold values from -6 to 6
- out_gain: float32 [2048], replicated, may hold values from 0.5 to 1.5
- doc_lengths: int32 [4, 12], P('dp'), may hold values from 1 to 341, 1024 in all within a row
Outputs:
- output: bfloat16 [4, 1024, 2048], P('dp', 'ctx')
- grad_queries: bfloat16 [4, 1024, 2048], P('dp', 'ctx')
- grad_keys: bfloat16 [4, 1024, 2048], P('dp', 'ctx')
- grad_values: bfloat16 [4, 1024, 2048], P('dp', 'ctx')
- grad_gain: float32 [2048], replicated
Inputs may be any that keep to these rules, and one draw needn't show every extreme that they name: `doc_lengths`: each row holds the lengths of 12 documents packed end to end; they sum to 1024, and the largest is exactly 341.
All inputs are finite; a program needn't handle non-finite values.
Results may differ from a plain program's by a relative error of at most 0.012.
The roundings to bfloat16 on the way count: a program that leaves them out, or rounds other values in their place, can miss the bound.
Values may be sent and summed in bfloat16 or wider, within the bound.
A program may use at most 64 MiB of HBM per device.

v0:
```python
import math

import jax
import jax.numpy as jnp
from jax import lax
from jax.sharding import PartitionSpec as P

H = 32
E = 64


eps = 1e-05


def entering(part, axis, combine, identity):
    place = lax.axis_index(axis)
    gathered = jax.tree.map(lambda a: lax.all_gather(a, axis), part)
    state = jax.tree.map(lambda a, e: jnp.zeros_like(a) + jnp.asarray(e, a.dtype), part, identity)

    def entering_one(step, state):
        return combine(
            state, jax.tree.map(lambda a: lax.dynamic_index_in_dim(a, step, 0, False), gathered)
        )

    return lax.fori_loop(0, place, entering_one, state)


def carried_in(shard, axis, join, neutral):
    count = lax.axis_size(axis)
    place = lax.axis_index(axis)
    ahead = count - 1 - place
    gathered = jax.tree.map(
        lambda a, kind: lax.all_gather(a.astype(kind), axis), shard, (jnp.bfloat16, jnp.bfloat16)
    )
    state = jax.tree.map(lambda a, e: jnp.zeros_like(a) + jnp.asarray(e, a.dtype), shard, neutral)

    def carried_one(step, state):
        source = count - 1 - step
        return join(
            state,
            jax.tree.map(
                lambda a, own: lax.dynamic_index_in_dim(a, source, 0, False).astype(own.dtype),
                gathered,
                shard,
            ),
        )

    return lax.fori_loop(0, ahead, carried_one, state)


def doc_geometry(doc_lengths, positions):
    doc_ends = jnp.cumsum(doc_lengths, axis=1)
    begins = doc_ends - doc_lengths
    doc_ids = jnp.sum((positions[None, :, None] >= doc_ends[:, None, :]).astype(jnp.int32), axis=2)
    starts = jnp.sum((positions[None, :, None] == begins[:, None, :]).astype(jnp.float32), axis=2)
    return (doc_ids, starts)


def chain_join(earlier, later):
    keep = (1.0 - later[1]).reshape((-1,) + (1,) * (later[0].ndim - 1))
    state_sum = later[0] + keep * earlier[0]
    return (state_sum, jnp.maximum(earlier[1], later[1]))


def split_product(form, data, state):
    high_part = state.astype(jnp.bfloat16)
    low_part = (state - lax.optimization_barrier(high_part).astype(jnp.float32)).astype(
        jnp.bfloat16
    )
    first = jnp.einsum(form, data, high_part, preferred_element_type=jnp.float32)
    return first + jnp.einsum(form, data, low_part, preferred_element_type=jnp.float32)


def blocks_math(
    queries, keys, values, grad_output, gain_heads, doc_ids, starts, forward_carry, backward_carry
):
    counted = jnp.cumsum(starts, axis=1)
    totals = counted[:, -1:]
    before = (counted == 0).astype(jnp.float32)[:, :, None, None]
    after_mask = (totals - counted == 0).astype(jnp.float32)[:, :, None, None]
    opened = jnp.minimum(totals[:, 0], 1.0)
    row_ids = jnp.arange(queries.shape[1])
    causal = row_ids[:, None] >= row_ids[None, :]
    doc_mask = jnp.logical_and(causal[None], doc_ids[:, :, None] == doc_ids[:, None, :]).astype(
        jnp.float32
    )[:, None]
    scores = jnp.einsum("btge,bsge->bgts", queries, keys, preferred_element_type=jnp.float32)
    weights = (scores * doc_mask).astype(jnp.bfloat16)
    own_state = jnp.einsum(
        "bsge,bsgf->bgef",
        keys * after_mask.astype(jnp.bfloat16),
        values,
        preferred_element_type=jnp.float32,
    )
    carried = forward_carry(own_state, opened)
    attended = jnp.einsum("bgts,bsgf->btgf", weights, values, preferred_element_type=jnp.float32)
    attended = attended + before * split_product("btge,bgef->btgf", queries, carried)
    root_mean = jnp.sqrt(jnp.mean(attended * attended, axis=-1, keepdims=True) + eps)
    normed = attended / root_mean
    output = (gain_heads * normed).astype(jnp.bfloat16)
    dyf = grad_output.astype(jnp.float32)
    dnormed = dyf * gain_heads
    grad_att = (
        (dnormed - normed * jnp.mean(dnormed * normed, axis=-1, keepdims=True)) / root_mean
    ).astype(jnp.bfloat16)
    gain_part = jnp.sum(dyf * normed, axis=(0, 1))
    grad_scores = jnp.einsum(
        "btgf,bsgf->bgts", grad_att, values, preferred_element_type=jnp.float32
    )
    grad_weights = (grad_scores * doc_mask).astype(jnp.bfloat16)
    back_state = jnp.einsum(
        "btge,btgf->bgef",
        queries * before.astype(jnp.bfloat16),
        grad_att,
        preferred_element_type=jnp.float32,
    )
    back_carried = backward_carry(back_state, opened)
    grad_q = jnp.einsum("bgts,bsge->btge", grad_weights, keys, preferred_element_type=jnp.float32)
    grad_q = grad_q + before * split_product("btgf,bgef->btge", grad_att, carried)
    grad_k = jnp.einsum(
        "bgts,btge->bsge", grad_weights, queries, preferred_element_type=jnp.float32
    )
    grad_k = grad_k + after_mask * split_product("bsgf,bgef->bsge", values, back_carried)
    grad_v = jnp.einsum("bgts,btgf->bsgf", weights, grad_att, preferred_element_type=jnp.float32)
    grad_v = grad_v + after_mask * split_product("bsge,bgef->bsgf", keys, back_carried)
    return (
        output,
        grad_q.astype(jnp.bfloat16),
        grad_k.astype(jnp.bfloat16),
        grad_v.astype(jnp.bfloat16),
        gain_part,
    )


def per_device(queries, keys, values, grad_output, out_gain, doc_lengths):
    local_seqs, block_len, width = queries.shape
    ctx_count = lax.axis_size("ctx")
    ctx_index = lax.axis_index("ctx")
    shape4 = (local_seqs, block_len, H, E)
    quad = tuple((item.reshape(shape4) for item in (queries, keys, values, grad_output)))
    gain_heads = out_gain.reshape(H, E)
    positions = ctx_index * block_len + jnp.arange(block_len, dtype=jnp.int32)
    doc_ids, starts = doc_geometry(doc_lengths, positions)

    def chain_forward(state, opened):
        wide = state.reshape(state.shape[0], H, E * E)
        moved = entering(
            (wide, opened), "ctx", chain_join, (jnp.zeros_like(wide), jnp.zeros_like(opened))
        )[0]
        return moved.reshape(state.shape)

    def chain_backward(state, opened):
        wide = state.reshape(state.shape[0], H, E * E)
        moved = carried_in(
            (wide, opened), "ctx", chain_join, (jnp.zeros_like(wide), jnp.zeros_like(opened))
        )[0]
        return moved.reshape(state.shape)

    results = blocks_math(
        quad[0],
        quad[1],
        quad[2],
        quad[3],
        gain_heads,
        doc_ids,
        starts,
        chain_forward,
        chain_backward,
    )
    returned = results[:4]
    gain_terms = results[4]
    total_tokens = local_seqs * lax.axis_size("dp") * block_len * ctx_count
    grad_gain = lax.psum(gain_terms.reshape(H * E), ("dp", "ctx")) / math.sqrt(total_tokens)
    flat = (local_seqs, block_len, H * E)
    outputs = tuple((item.reshape(flat) for item in returned))
    return (outputs[0], outputs[1], outputs[2], outputs[3], grad_gain)


def solution(mesh):
    placed = (
        P("dp", "ctx", None),
        P("dp", "ctx", None),
        P("dp", "ctx", None),
        P("dp", "ctx", None),
        P(),
        P("dp", None),
    )
    return jax.shard_map(
        per_device,
        mesh=mesh,
        in_specs=placed,
        out_specs=(
            P("dp", "ctx", None),
            P("dp", "ctx", None),
            P("dp", "ctx", None),
            P("dp", "ctx", None),
            P(),
        ),
        check_vma=False,
    )
```

profile of v0, /device:TPU:0, one launch (start us, length us, event | category | flops | bytes accessed | tf_op | source)
XLA Modules:
  0.0 177.1 jit_solution(15411295630107425023)
XLA Ops:
  7.2 1.3 copy.67
  8.5 1.3 copy.66
  10.2 0.3 reduce_window_sum.23
  10.5 0.6 slice.3
  11.1 0.6 fusion.40
  11.8 0.4 fusion.25
  12.2 1.2 all_gather_reshape.3
  14.1 0.6 dynamic-slice
  14.7 0.7 bitcast_dynamic-update-slice_fusion
  15.3 15.3 %all-reduce = f32[8]{0:T(128)S(1)} all-reduce(f32[8]{0:T(128)S(1)} %bitcast_dynamic-update-slice_fusion), channel_id=1, replica_groups=mesh['dp'=4,'ctx'=8] {'ctx'}, use_global_device_ids=true, to_apply=%add | all-reduce | flops 8 | bytes 64
  30.7 1.2 copy.70
  32.5 0.5 multiply_convert_fusion.1
  33.0 20.0 %all-gather.3.cloned.1.call-done = f32[8,1,32,4096]{3,2,1,0:T(8,128)} async-done(((f32[1,1,32,4096]{3,2,1,0:T(8,128)}), f32[8,1,32,4096]{3,2,1,0:T(8,128)}) %all-gather.3.cloned.1.call-update) | async-done | bytes 4194320 | tf_op jit(solution)/shard_map/all_gather | solution.py:17
  53.1 1.4 reshape.498
  54.5 0.5 convert_element_type.238
  55.0 0.3 fusion.44
  55.4 0.9 copy-done
  56.3 0.4 fusion.9
  56.7 0.4 copy-done.7
  57.1 0.8 multiply_reduce_fusion.2
  58.0 0.4 copy-done.6
  58.4 0.8 multiply_reduce_fusion
  59.2 0.5 divide_convert_fusion
  59.7 1.2 convolution_convert_fusion
  60.9 2.2 %convert_element_type.251 = bf16[1,1,32,4096]{3,2,1,0:T(8,128)(2,1)} reshape(bf16[32,64,64]{2,1,0:T(8,128)(2,1)} %convolution_convert_fusion) | data formatting | bytes 524288 | tf_op jit(solution)/shard_map/convert_element_type | solution.py:33
  63.1 0.8 dynamic-update-slice.1
  63.9 30.6 %all-reduce.1 = bf16[8]{0:T(256)(128)(2,1)S(1)} all-reduce(bf16[8]{0:T(256)(128)(2,1)S(1)} %dynamic-update-slice.1), channel_id=1, replica_groups=mesh['dp'=4,'ctx'=8] {'ctx'}, use_global_device_ids=true, to_apply=%add.1 | all-reduce | flops 8 | bytes 32
  94.5 1.0 copy.75
  95.8 0.5 multiply_convert_fusion
  96.3 0.4 copy-done.1
  96.9 0.3 fusion.10
  97.2 0.7 copy-done.4
  97.9 0.8 fusion.13
  98.7 1.0 copy.76
  99.8 39.4 %psum.7 = f32[2048]{0:T(1024)S(1)} all-reduce(f32[2048]{0:T(1024)S(1)} %reshape.507), channel_id=1, replica_groups=mesh['dp'=4,'ctx'=8] {'dp','ctx'}, use_global_device_ids=true, to_apply=%region_11.12 | all-reduce | flops 2048 | bytes 16384 | tf_op jit(solution)/shard_map/psum | solution.py:173
  139.1 0.6 broadcast_multiply_fusion.1
  139.8 17.0 %while.27 = (s32[]{:T(128)}, f32[1,32,4096]{2,1,0:T(8,128)S(1)}, s32[]{:T(128)}, bf16[8,1,32,4096]{3,2,1,0:T(8,128)(2,1)}, bf16[8,1]{0,1:T(2,128)(2,1)S(1)}, /*index=5*/s32[]{:T(128)}, s32[]{:T(128)}, s32[]{:T(128)}, s32[]{:T(128)}) while((s32[]{:T(128)}, f32[1,32,4096]{2,1,0:T(8,128)S(1)}, s32[]{:T(128)}, ...), condition=%wide.region_9.10_spmd, body=%wide.region_8.9_spmd.sunk | while | flops 393223 | bytes 1310885 | solution.py:48
  139.8 0.6 fusion.71
  140.4 1.8 %convert_add_fusion.2 = f32[1,32,4096]{2,1,0:T(8,128)S(1)} fusion(f32[1,32,4096]{2,1,0:T(8,128)S(1)} %get-tuple-element.283, f32[]{:T(128)} %bitcast.135, bf16[8,1,32,4096]{3,2,1,0:T(8,128)(2,1)} %get-tuple-element.294, s32[]{:T(128)S(6)} %select_n.20), kind=kLoop, calls=%fused_computation.2.clone.1 | loop fusion | flops 393216 | bytes 1310728 | tf_op jit(solution)/shard_map/while/body/add | solution.py:61
  142.2 0.6 fusion.71
  142.8 1.8 %convert_add_fusion.2 = f32[1,32,4096]{2,1,0:T(8,128)S(1)} fusion(f32[1,32,4096]{2,1,0:T(8,128)S(1)} %get-tuple-element.283, f32[]{:T(128)} %bitcast.135, bf16[8,1,32,4096]{3,2,1,0:T(8,128)(2,1)} %get-tuple-element.294, s32[]{:T(128)S(6)} %select_n.20), kind=kLoop, calls=%fused_computation.2.clone.1 | loop fusion | flops 393216 | bytes 1310728 | tf_op jit(solution)/shard_map/while/body/add | solution.py:61
  144.6 0.6 fusion.71
  145.2 1.8 %convert_add_fusion.2 = f32[1,32,4096]{2,1,0:T(8,128)S(1)} fusion(f32[1,32,4096]{2,1,0:T(8,128)S(1)} %get-tuple-element.283, f32[]{:T(128)} %bitcast.135, bf16[8,1,32,4096]{3,2,1,0:T(8,128)(2,1)} %get-tuple-element.294, s32[]{:T(128)S(6)} %select_n.20), kind=kLoop, calls=%fused_computation.2.clone.1 | loop fusion | flops 393216 | bytes 1310728 | tf_op jit(solution)/shard_map/while/body/add | solution.py:61
  147.0 0.6 fusion.71
  147.6 1.8 %convert_add_fusion.2 = f32[1,32,4096]{2,1,0:T(8,128)S(1)} fusion(f32[1,32,4096]{2,1,0:T(8,128)S(1)} %get-tuple-element.283, f32[]{:T(128)} %bitcast.135, bf16[8,1,32,4096]{3,2,1,0:T(8,128)(2,1)} %get-tuple-element.294, s32[]{:T(128)S(6)} %select_n.20), kind=kLoop, calls=%fused_computation.2.clone.1 | loop fusion | flops 393216 | bytes 1310728 | tf_op jit(solution)/shard_map/while/body/add | solution.py:61
  149.4 0.6 fusion.71
  150.0 1.8 %convert_add_fusion.2 = f32[1,32,4096]{2,1,0:T(8,128)S(1)} fusion(f32[1,32,4096]{2,1,0:T(8,128)S(1)} %get-tuple-element.283, f32[]{:T(128)} %bitcast.135, bf16[8,1,32,4096]{3,2,1,0:T(8,128)(2,1)} %get-tuple-element.294, s32[]{:T(128)S(6)} %select_n.20), kind=kLoop, calls=%fused_computation.2.clone.1 | loop fusion | flops 393216 | bytes 1310728 | tf_op jit(solution)/shard_map/while/body/add | solution.py:61
  151.8 0.6 fusion.71
  152.4 1.8 %convert_add_fusion.2 = f32[1,32,4096]{2,1,0:T(8,128)S(1)} fusion(f32[1,32,4096]{2,1,0:T(8,128)S(1)} %get-tuple-element.283, f32[]{:T(128)} %bitcast.135, bf16[8,1,32,4096]{3,2,1,0:T(8,128)(2,1)} %get-tuple-element.294, s32[]{:T(128)S(6)} %select_n.20), kind=kLoop, calls=%fused_computation.2.clone.1 | loop fusion | flops 393216 | bytes 1310728 | tf_op jit(solution)/shard_map/while/body/add | solution.py:61
  154.2 0.6 fusion.71
  154.8 1.8 %convert_add_fusion.2 = f32[1,32,4096]{2,1,0:T(8,128)S(1)} fusion(f32[1,32,4096]{2,1,0:T(8,128)S(1)} %get-tuple-element.283, f32[]{:T(128)} %bitcast.135, bf16[8,1,32,4096]{3,2,1,0:T(8,128)(2,1)} %get-tuple-element.294, s32[]{:T(128)S(6)} %select_n.20), kind=kLoop, calls=%fused_computation.2.clone.1 | loop fusion | flops 393216 | bytes 1310728 | tf_op jit(solution)/shard_map/while/body/add | solution.py:61
  156.8 1.5 reshape.503
  158.3 0.5 convert_element_type.254
  158.8 1.3 fusion.45
  160.1 1.3 fusion.46
  161.4 1.6 copy.72
  163.1 1.3 copy-done.10
  164.4 0.4 fusion.11
  164.8 0.8 copy-done.5
  165.6 0.4 fusion.14
  166.0 1.0 copy.77
  167.0 1.8 fusion.12
  168.8 0.4 fusion.15
  169.2 1.0 copy.78
  (51 shorter events, 1.8 us)
Async XLA Ops:
  7.2 2.7 %copy-start.14 = (s32[1,12]{1,0:T(1,128)S(1)}, s32[1,12]{1,0:T(1,128)}, u32[]{:S(2)}) copy-start(s32[1,12]{1,0:T(1,128)} %param.15) | copy-start | bytes 148
  7.2 45.8 %all-gather.3.cloned.1.call-start = ((), (), s32[]{:S(2)}) async-start(), calls=%async_computation | async-start | bytes 4718592 | tf_op jit(solution)/shard_map/all_gather | solution.py:17
  11.7 2.3 %copy-start.15 = (u32[32]{0:T(128)S(1)}, u32[32]{0:T(128)}, u32[]{:S(2)}) copy-start(u32[32]{0:T(128)} %constant.97) | copy-start | bytes 388
  11.8 18.9 %copy-start.11 = (bf16[1,128,2048]{2,1,0:T(8,128)(2,1)S(1)}, bf16[1,128,2048]{2,1,0:T(8,128)(2,1)}, u32[]{:S(2)}) copy-start(bf16[1,128,2048]{2,1,0:T(8,128)(2,1)} %param.13) | copy-start | bytes 1572868
  12.2 19.7 %copy-start.12 = (bf16[1,128,2048]{2,1,0:T(8,128)(2,1)S(1)}, bf16[1,128,2048]{2,1,0:T(8,128)(2,1)}, u32[]{:S(2)}) copy-start(bf16[1,128,2048]{2,1,0:T(8,128)(2,1)} %param.10) | copy-start | bytes 1572868
  12.2 20.0 %copy-start.13 = (f32[2048]{0:T(1024)S(1)}, f32[2048]{0:T(1024)}, u32[]{:S(2)}) copy-start(f32[2048]{0:T(1024)} %param.14) | copy-start | bytes 24580
  13.4 126.4 %all-gather.5.cloned.1.call-start = ((), (), s32[]{:S(2)}) async-start(), calls=%async_computation.1 | async-start | bytes 2359296 | tf_op jit(solution)/shard_map/all_gather | solution.py:33
  33.0 23.8 %copy-start.2 = (bf16[32,128,128]{2,1,0:T(8,128)(2,1)}, bf16[32,128,128]{2,1,0:T(8,128)(2,1)S(1)}, u32[]{:S(2)}) copy-start(bf16[32,128,128]{2,1,0:T(8,128)(2,1)S(1)} %multiply_convert_fusion.1) | copy-start | bytes 3145732
  55.0 1.2 copy-start
  56.3 0.8 copy-start.7
  57.1 1.2 copy-start.6
  95.5 1.2 copy-start.1
  95.5 1.4 copy-start.8
  96.9 1.0 copy-start.4
  163.0 1.4 copy-start.10
  163.1 1.7 copy-start.9
  164.4 1.2 copy-start.5
  167.0 1.8 copy-start.3
Sparse Core Ops, SparseCore 0:
  13.5 39.4 all-gather.2
  63.2 45.6 all-gather.4
where the time goes:
time: 178 us; the launch traced here: 177 us
  blocking collectives  85.3 us (48%)
  local copies, waits for them, and re-layouts  24.9 us (14%)
  other arithmetic  20.2 us (11%)
  waiting for transfers between devices  20 us (11%)
  between operations  15.1 us (8%)
  matrix products  11.1 us (6%)
    unnamed x2, blocking collectives  46 us
    psum x1, blocking collectives, per_device(): lax.psum(gain_terms.reshape(H * E), ('dp', 'ctx')) / math.sqrt(total_tokens)  39.4 us
    all_gather x1, waiting for transfers between devices, entering(): gathered = jax.tree.map(lambda a: lax.all_gather(a, axis), part)  20 us
    unnamed x44, local copies, waits for them, and re-layouts  14 us
    add x7, other arithmetic, chain_join(): state_sum = later[0] + keep * earlier[0]  12.5 us
    sub x7, other arithmetic, chain_join(): keep = (1.0 - later[1]).reshape((-1,) + (1,) * (later[0].ndim - 1))  4.1 us
  transfers between devices with their start and end apart: 2, of which 1 were waited for; matrix products, arithmetic and copies ran while one was open for 5% of the time, Pallas kernels for 0%

commit v1 on v0

v1 whole, which is shorter than its diff:
```python
import functools
import math

import jax
import jax.numpy as jnp
from jax import lax
from jax.experimental import pallas as pl
from jax.experimental.pallas import tpu as pltpu
from jax.sharding import PartitionSpec as P

H = 32
E = 64
LANES = 2 * E
PAIRS = H // 2
CHUNKS = 4
PER = PAIRS // CHUNKS
EPS = 1e-05
BF = jnp.bfloat16
F32 = jnp.float32


def nn(a, b):
    return lax.dot_general(a, b, (((1,), (0,)), ((), ())), preferred_element_type=F32)


def nt(a, b):
    return lax.dot_general(a, b, (((1,), (1,)), ((), ())), preferred_element_type=F32)


def tn(a, b):
    return lax.dot_general(a, b, (((0,), (0,)), ((), ())), preferred_element_type=F32)


def kernel(
    n_ctx, n_dp, reach, total_tokens,
    lengths_ref, q_ref, k_ref, v_ref, dy_ref, gain_ref,
    out_ref, gq_ref, gk_ref, gv_ref, gg_ref,
    masks, doc_mask, own, back, fbuf, bbuf, carried, weights, att_s, gatt_s, gk_s, gv_s,
    gain_ctx, gain_dp,
    fsend, frecv, bsend, brecv, gsend, grecv, hsend, hrecv,
):
    me = lax.axis_index("ctx")
    mydp = lax.axis_index("dp")
    T = q_ref.shape[1]

    barrier = pltpu.get_barrier_semaphore()
    for d in range(1, n_ctx):
        pl.semaphore_signal(barrier, inc=1, device_id={"ctx": lax.rem(me + d, n_ctx)})
    for d in range(1, n_dp):
        pl.semaphore_signal(barrier, inc=1, device_id={"dp": lax.rem(mydp + d, n_dp)})

    docs = lengths_ref.shape[1]
    offset = me * T
    first, last = jnp.int32(1 << 20), jnp.int32(-(1 << 20))
    hits_f = [jnp.int32(0)] * (reach + 1)
    hits_b = [jnp.int32(0)] * (reach + 1)
    row = lax.broadcasted_iota(jnp.int32, (T, T), 0)
    col = lax.broadcasted_iota(jnp.int32, (T, T), 1)
    id_row = jnp.zeros((T, T), jnp.int32)
    id_col = jnp.zeros((T, T), jnp.int32)
    begin = -offset
    for i in range(docs):
        first = jnp.where(begin >= 0, jnp.minimum(first, begin), first)
        last = jnp.where(begin < T, jnp.maximum(last, begin), last)
        for d in range(2, reach + 1):
            hits_f[d] += jnp.where((begin >= -(d - 1) * T) & (begin < 0), 1, 0)
            hits_b[d] += jnp.where((begin >= T) & (begin < d * T), 1, 0)
        id_row += (row >= begin).astype(jnp.int32)
        id_col += (col >= begin).astype(jnp.int32)
        begin = begin + lengths_ref[0, i]
    coef_f = [jnp.where(hits_f[d] == 0, 1.0, 0.0).astype(F32) for d in range(reach + 1)]
    coef_b = [jnp.where(hits_b[d] == 0, 1.0, 0.0).astype(F32) for d in range(reach + 1)]
    dm = jnp.where((row >= col) & (id_row == id_col), 1.0, 0.0).astype(BF)
    doc_mask[0:T] = dm
    doc_mask[T:2 * T] = dm
    trow = lax.broadcasted_iota(jnp.int32, (T, LANES), 0)
    lane = lax.broadcasted_iota(jnp.int32, (T, LANES), 1)
    masks[0] = jnp.where(lane < E, 1.0, 0.0).astype(BF)
    masks[1] = jnp.where(lane < E, 0.0, 1.0).astype(BF)
    masks[2] = jnp.where(trow < first, 1.0, 0.0).astype(BF)
    masks[3] = jnp.where(trow >= last, 1.0, 0.0).astype(BF)

    for d in range(1, reach + 1):
        @pl.when(me - d < 0)
        def _():
            fbuf[d - 1] = jnp.zeros(fbuf.shape[1:], BF)

        @pl.when(me + d >= n_ctx)
        def _():
            bbuf[d - 1] = jnp.zeros(bbuf.shape[1:], BF)

    def lanes(p):
        return pl.ds(pl.multiple_of(p * LANES, LANES), LANES)

    def compact(full):
        left = lax.broadcasted_iota(jnp.int32, (E, LANES), 1) < E
        return jnp.where(left, full[:E], full[E:]).astype(BF)

    def diag(c):
        return jnp.concatenate([c * masks[0, 0:E], c * masks[1, 0:E]], axis=0)

    def stack(x):
        return jnp.concatenate([x * masks[0], x * masks[1]], axis=0)

    def fcopy(d, c):
        part = pl.ds(c * PER, PER)
        return pltpu.make_async_remote_copy(
            src_ref=own.at[part], dst_ref=fbuf.at[d - 1, part],
            send_sem=fsend.at[d - 1, c], recv_sem=frecv.at[d - 1, c],
            device_id={"ctx": lax.rem(me + d, n_ctx)},
        )

    def bcopy(d, c):
        part = pl.ds(c * PER, PER)
        return pltpu.make_async_remote_copy(
            src_ref=back.at[part], dst_ref=bbuf.at[d - 1, part],
            send_sem=bsend.at[d - 1, c], recv_sem=brecv.at[d - 1, c],
            device_id={"ctx": lax.rem(me - d + n_ctx, n_ctx)},
        )

    def loop(lo, hi, body):
        def step(p, _):
            body(p)
            return 0
        lax.fori_loop(lo, hi, step, 0)

    def state_of(p):
        own[p] = compact(tn(k_ref[0, :, lanes(p)] * masks[3], v_ref[0, :, lanes(p)]))

    for c in range(CHUNKS):
        loop(c * PER, (c + 1) * PER, state_of)
        if c == 0:
            pl.semaphore_wait(barrier, n_ctx + n_dp - 2)
        for d in range(1, reach + 1):
            @pl.when(me + d < n_ctx)
            def _():
                fcopy(d, c).start()

    def inside(p):
        q, k, v = q_ref[0, :, lanes(p)], k_ref[0, :, lanes(p)], v_ref[0, :, lanes(p)]
        w = nt(stack(q), k).astype(BF) * doc_mask[...]
        weights[p] = w
        att_s[p] = nn(jnp.concatenate([w[:T], w[T:]], axis=1), stack(v))

    loop(0, PAIRS, inside)

    jrow = lax.broadcasted_iota(jnp.int32, (2 * LANES, LANES), 0)
    jlane = lax.broadcasted_iota(jnp.int32, (2 * LANES, LANES), 1)
    mean_of = jnp.where((lax.rem(jrow, LANES) < E) == (jlane < E), 1.0 / E, 0.0).astype(BF)

    def head_mean(x):
        high = x.astype(BF)
        low = (x - high.astype(F32)).astype(BF)
        return nn(jnp.concatenate([high, low], axis=1), mean_of)

    def normalize(p):
        c = fbuf[0, p].astype(F32) * coef_f[1]
        for d in range(2, reach + 1):
            c += fbuf[d - 1, p].astype(F32) * coef_f[d]
        c = c.astype(BF)
        carried[p] = c
        qb = q_ref[0, :, lanes(p)] * masks[2]
        att = att_s[p] + nn(qb, diag(c))
        inv = lax.rsqrt(head_mean(att * att) + EPS)
        normed = att * inv
        gain = gain_ref[:, lanes(p)]
        out_ref[0, :, lanes(p)] = (gain * normed).astype(BF)
        dy = dy_ref[0, :, lanes(p)].astype(F32)
        dn = dy * gain
        gatt = ((dn - normed * head_mean(dn * normed)) * inv).astype(BF)
        gatt_s[p] = gatt
        gain_ctx[me, pl.ds(p, 1)] = jnp.sum(dy * normed, axis=0, keepdims=True)
        back[p] = compact(tn(qb, gatt))

    for c in range(CHUNKS):
        for d in range(1, reach + 1):
            @pl.when(me - d >= 0)
            def _():
                fcopy(d, c).wait_recv()
        loop(c * PER, (c + 1) * PER, normalize)
        for d in range(1, reach + 1):
            @pl.when(me - d >= 0)
            def _():
                bcopy(d, c).start()

    def gcopy(d, slot):
        return pltpu.make_async_remote_copy(
            src_ref=gain_ctx.at[slot], dst_ref=gain_ctx.at[slot],
            send_sem=gsend.at[d - 1], recv_sem=grecv.at[d - 1],
            device_id={"ctx": lax.rem(me + d, n_ctx)},
        )

    def hcopy(d, slot):
        return pltpu.make_async_remote_copy(
            src_ref=gain_dp.at[slot], dst_ref=gain_dp.at[slot],
            send_sem=hsend.at[d - 1], recv_sem=hrecv.at[d - 1],
            device_id={"dp": lax.rem(mydp + d, n_dp)},
        )

    for d in range(1, n_ctx):
        gcopy(d, me).start()

    def gradients(p):
        q, k, v = q_ref[0, :, lanes(p)], k_ref[0, :, lanes(p)], v_ref[0, :, lanes(p)]
        gatt = gatt_s[p]
        gs = stack(gatt)
        gw = nt(gs, v).astype(BF) * doc_mask[...]
        gq = nn(jnp.concatenate([gw[:T], gw[T:]], axis=1), stack(k))
        gq += nt(gatt * masks[2], diag(carried[p]))
        gq_ref[0, :, lanes(p)] = gq.astype(BF)
        gk_s[p] = tn(gw, stack(q))
        gv_s[p] = tn(weights[p], gs)

    loop(0, PAIRS, gradients)

    for d in range(1, n_ctx):
        gcopy(d, lax.rem(me - d + n_ctx, n_ctx)).wait_recv()
    total = gain_ctx[0]
    for i in range(1, n_ctx):
        total += gain_ctx[i]
    gain_dp[mydp] = total
    for d in range(1, n_dp):
        hcopy(d, mydp).start()

    def finish(p):
        c = bbuf[0, p].astype(F32) * coef_b[1]
        for d in range(2, reach + 1):
            c += bbuf[d - 1, p].astype(F32) * coef_b[d]
        bd = diag(c.astype(BF))
        after = masks[3]
        gk_ref[0, :, lanes(p)] = (gk_s[p] + nt(v_ref[0, :, lanes(p)] * after, bd)).astype(BF)
        gv_ref[0, :, lanes(p)] = (gv_s[p] + nn(k_ref[0, :, lanes(p)] * after, bd)).astype(BF)

    for c in range(CHUNKS):
        for d in range(1, reach + 1):
            @pl.when(me + d < n_ctx)
            def _():
                bcopy(d, c).wait_recv()
        loop(c * PER, (c + 1) * PER, finish)

    for d in range(1, n_dp):
        hcopy(d, lax.rem(mydp - d + n_dp, n_dp)).wait_recv()
    total = gain_dp[0]
    for i in range(1, n_dp):
        total += gain_dp[i]
    gg_ref[...] = total * (1.0 / math.sqrt(total_tokens))

    for c in range(CHUNKS):
        for d in range(1, reach + 1):
            @pl.when(me + d < n_ctx)
            def _():
                fcopy(d, c).wait_send()

            @pl.when(me - d >= 0)
            def _():
                bcopy(d, c).wait_send()
    for d in range(1, n_ctx):
        gcopy(d, me).wait_send()
    for d in range(1, n_dp):
        hcopy(d, mydp).wait_send()


def per_device(queries, keys, values, grad_output, out_gain, doc_lengths):
    _, T, width = queries.shape
    n_ctx, n_dp = lax.axis_size("ctx"), lax.axis_size("dp")
    length = T * n_ctx
    longest = length // 3
    reach = min(n_ctx - 1, -(-(longest - 1) // T))
    vmem = pl.BlockSpec(memory_space=pltpu.VMEM)
    data = jax.ShapeDtypeStruct((1, T, width), BF)
    dma = pltpu.SemaphoreType.DMA
    out = pl.pallas_call(
        functools.partial(kernel, n_ctx, n_dp, reach, n_dp * length),
        out_shape=(data,) * 4 + (jax.ShapeDtypeStruct((PAIRS, LANES), F32),),
        in_specs=[pl.BlockSpec(memory_space=pltpu.SMEM)] + [vmem] * 5,
        out_specs=(vmem,) * 5,
        scratch_shapes=[
            pltpu.VMEM((4, T, LANES), BF),
            pltpu.VMEM((2 * T, T), BF),
            pltpu.VMEM((PAIRS, E, LANES), BF),
            pltpu.VMEM((PAIRS, E, LANES), BF),
            pltpu.VMEM((reach, PAIRS, E, LANES), BF),
            pltpu.VMEM((reach, PAIRS, E, LANES), BF),
            pltpu.VMEM((PAIRS, E, LANES), BF),
            pltpu.VMEM((PAIRS, 2 * T, T), BF),
            pltpu.VMEM((PAIRS, T, LANES), F32),
            pltpu.VMEM((PAIRS, T, LANES), BF),
            pltpu.VMEM((PAIRS, T, LANES), F32),
            pltpu.VMEM((PAIRS, T, LANES), F32),
            pltpu.VMEM((n_ctx, PAIRS, LANES), F32),
            pltpu.VMEM((n_dp, PAIRS, LANES), F32),
            dma((reach, CHUNKS)), dma((reach, CHUNKS)),
            dma((reach, CHUNKS)), dma((reach, CHUNKS)),
            dma((n_ctx - 1,)), dma((n_ctx - 1,)),
            dma((n_dp - 1,)), dma((n_dp - 1,)),
        ],
        compiler_params=pltpu.CompilerParams(
            collective_id=0, has_side_effects=True, vmem_limit_bytes=48 * 1024 * 1024
        ),
    )(doc_lengths, queries, keys, values, grad_output, out_gain.reshape(1, width))
    return (*out[:4], out[4].reshape(width))


def solution(mesh):
    seq = P("dp", "ctx", None)
    return jax.shard_map(
        per_device,
        mesh=mesh,
        in_specs=(seq, seq, seq, seq, P(), P("dp", None)),
        out_specs=(seq, seq, seq, seq, P()),
        check_vma=False,
    )
```

time: 178 us -> 48.3 us (0.27)
  the two profiles are of different devices: /device:TPU:0 before, /device:TPU:4 now
where the time goes in v1:
time: 48.3 us; the launch traced here: 47.9 us
  Pallas kernels  38 us (79%)
  local copies, waits for them, and re-layouts  9.28 us (19%)
  between operations  0.66 us (1%)
    pallas_call x1, Pallas kernels, per_device(): pl.pallas_call(functools.partial(kernel, n_ctx, n_dp, reach, n_dp * lengt...  38 us
    unnamed x17, local copies, waits for them, and re-layouts  9.28 us

profile of v1, /device:TPU:4, one launch (start us, length us, event | category | flops | bytes accessed | tf_op | source)
XLA Modules:
  0.0 47.9 jit_solution(7264231586245871304)
XLA Ops:
  0.6 0.0 copy-start.5
  0.6 0.6 %copy-done.5 = s32[1,12]{1,0:T(1,128)S(1)} copy-done((s32[1,12]{1,0:T(1,128)S(1)}, s32[1,12]{1,0:T(1,128)}, u32[]{:S(2)}) %copy-start.5) | copy-done | bytes 72
  1.3 0.0 copy-start
  1.3 1.0 %copy-done = bf16[1,128,2048]{2,1,0:T(8,128)(2,1)S(1)} copy-done((bf16[1,128,2048]{2,1,0:T(8,128)(2,1)S(1)}, bf16[1,128,2048]{2,1,0:T(8,128)(2,1)}, u32[]{:S(2)}) %copy-start) | copy-done | bytes 524312
  2.3 0.0 copy-start.1
  2.3 1.0 %copy-done.1 = bf16[1,128,2048]{2,1,0:T(8,128)(2,1)S(1)} copy-done((bf16[1,128,2048]{2,1,0:T(8,128)(2,1)S(1)}, bf16[1,128,2048]{2,1,0:T(8,128)(2,1)}, u32[]{:S(2)}) %copy-start.1) | copy-done | bytes 524312
  3.4 0.0 copy-start.2
  3.4 1.0 %copy-done.2 = bf16[1,128,2048]{2,1,0:T(8,128)(2,1)S(1)} copy-done((bf16[1,128,2048]{2,1,0:T(8,128)(2,1)S(1)}, bf16[1,128,2048]{2,1,0:T(8,128)(2,1)}, u32[]{:S(2)}) %copy-start.2) | copy-done | bytes 524312
  4.4 0.0 copy-start.3
  4.4 1.0 %copy-done.3 = bf16[1,128,2048]{2,1,0:T(8,128)(2,1)S(1)} copy-done((bf16[1,128,2048]{2,1,0:T(8,128)(2,1)S(1)}, bf16[1,128,2048]{2,1,0:T(8,128)(2,1)}, u32[]{:S(2)}) %copy-start.3) | copy-done | bytes 524312
  5.5 0.0 copy-start.4
  5.5 0.7 %copy-done.4 = f32[2048]{0:T(1024)S(1)} copy-done((f32[2048]{0:T(1024)S(1)}, f32[2048]{0:T(1024)}, u32[]{:S(2)}) %copy-start.4) | copy-done | bytes 8216
  6.2 38.0 %shard_map.101 = (bf16[1,128,2048]{2,1,0:T(8,128)(2,1)S(1)}, bf16[1,128,2048]{2,1,0:T(8,128)(2,1)S(1)}, bf16[1,128,2048]{2,1,0:T(8,128)(2,1)S(1)}, bf16[1,128,2048]{2,1,0:T(8,128)(2,1)S(1)}, f32[16,128]{1,0:T(8,128)S(1)}) custom-call(s32[1,12]{1,0:T(1,128)S(1)} %copy-done.5, bf16[1,128,2048]{2,1,0:T(8,128)(2,1)S(1)} %copy-done, ...), custom_call_target="tpu_custom_call" | custom-call | tf_op jit(solution)/shard_map/pallas_call | solution.py:272
  44.2 0.8 %copy.16 = bf16[1,128,2048]{2,1,0:T(8,128)(2,1)} copy(bf16[1,128,2048]{2,1,0:T(8,128)(2,1)S(1)} %get-tuple-element.20) | data formatting | bytes 1048576
  45.0 0.8 %copy.17 = bf16[1,128,2048]{2,1,0:T(8,128)(2,1)} copy(bf16[1,128,2048]{2,1,0:T(8,128)(2,1)S(1)} %get-tuple-element.21) | data formatting | bytes 1048576
  45.7 0.8 %copy.18 = bf16[1,128,2048]{2,1,0:T(8,128)(2,1)} copy(bf16[1,128,2048]{2,1,0:T(8,128)(2,1)S(1)} %get-tuple-element.22) | data formatting | bytes 1048576
  46.5 0.8 %copy.19 = bf16[1,128,2048]{2,1,0:T(8,128)(2,1)} copy(bf16[1,128,2048]{2,1,0:T(8,128)(2,1)S(1)} %get-tuple-element.23) | data formatting | bytes 1048576
  47.3 0.6 %copy.20 = f32[2048]{0:T(1024)} copy(f32[2048]{0:T(1024)S(1)} %bitcast.3) | data formatting | bytes 16384
Async XLA Ops:
  0.6 0.7 %copy-start.5 = (s32[1,12]{1,0:T(1,128)S(1)}, s32[1,12]{1,0:T(1,128)}, u32[]{:S(2)}) copy-start(s32[1,12]{1,0:T(1,128)} %lengths_ref.1) | copy-start | bytes 148
  1.3 1.0 %copy-start = (bf16[1,128,2048]{2,1,0:T(8,128)(2,1)S(1)}, bf16[1,128,2048]{2,1,0:T(8,128)(2,1)}, u32[]{:S(2)}) copy-start(bf16[1,128,2048]{2,1,0:T(8,128)(2,1)} %q_ref.1) | copy-start | bytes 1572868
  2.3 1.0 %copy-start.1 = (bf16[1,128,2048]{2,1,0:T(8,128)(2,1)S(1)}, bf16[1,128,2048]{2,1,0:T(8,128)(2,1)}, u32[]{:S(2)}) copy-start(bf16[1,128,2048]{2,1,0:T(8,128)(2,1)} %k_ref.1) | copy-start | bytes 1572868
  3.4 1.0 %copy-start.2 = (bf16[1,128,2048]{2,1,0:T(8,128)(2,1)S(1)}, bf16[1,128,2048]{2,1,0:T(8,128)(2,1)}, u32[]{:S(2)}) copy-start(bf16[1,128,2048]{2,1,0:T(8,128)(2,1)} %v_ref.1) | copy-start | bytes 1572868
  4.4 1.0 %copy-start.3 = (bf16[1,128,2048]{2,1,0:T(8,128)(2,1)S(1)}, bf16[1,128,2048]{2,1,0:T(8,128)(2,1)}, u32[]{:S(2)}) copy-start(bf16[1,128,2048]{2,1,0:T(8,128)(2,1)} %dy_ref.1) | copy-start | bytes 1572868
  5.5 0.7 %copy-start.4 = (f32[2048]{0:T(1024)S(1)}, f32[2048]{0:T(1024)}, u32[]{:S(2)}) copy-start(f32[2048]{0:T(1024)} %param.10) | copy-start | bytes 24580

commit v2 on v1

--- a/solution.py
+++ b/solution.py
@@ -15,6 +15,7 @@
 CHUNKS = 4
 PER = PAIRS // CHUNKS
 EPS = 1e-05
+VMEM_LIMIT = 58 * 1024 * 1024
 BF = jnp.bfloat16
 F32 = jnp.float32
 
@@ -33,8 +34,10 @@
 
 def kernel(
     n_ctx, n_dp, reach, total_tokens,
-    lengths_ref, q_ref, k_ref, v_ref, dy_ref, gain_ref,
-    out_ref, gq_ref, gk_ref, gv_ref, gg_ref,
+    lengths_hbm, q_hbm, k_hbm, v_hbm, dy_hbm, gain_hbm,
+    out_hbm, gq_hbm, gk_hbm, gv_hbm, gg_hbm,
+    lengths_ref, q_ref, k_ref, v_ref, dy_ref, gain_ref, in_sem, small_sem,
+    out_ref, gq_ref, gk_ref, gv_ref, gg_ref, out_sem, gg_sem,
     masks, doc_mask, own, back, fbuf, bbuf, carried, weights, att_s, gatt_s, gk_s, gv_s,
     gain_ctx, gain_dp,
     fsend, frecv, bsend, brecv, gsend, grecv, hsend, hrecv,
@@ -43,12 +46,44 @@
     mydp = lax.axis_index("dp")
     T = q_ref.shape[1]
 
+    small = [
+        pltpu.make_async_copy(lengths_hbm, lengths_ref, small_sem.at[0]),
+        pltpu.make_async_copy(gain_hbm, gain_ref, small_sem.at[1]),
+    ]
+
+    def incopy(i, c):
+        source, target = ((k_hbm, k_ref), (v_hbm, v_ref), (q_hbm, q_ref), (dy_hbm, dy_ref))[i]
+        part = pl.ds(pl.multiple_of(c * (PER * LANES), PER * LANES), PER * LANES)
+        return pltpu.make_async_copy(
+            source.at[:, :, part], target.at[:, :, part], in_sem.at[i, c]
+        )
+
+    def outcopy(i, c):
+        source, target = (
+            (out_ref, out_hbm), (gq_ref, gq_hbm), (gk_ref, gk_hbm), (gv_ref, gv_hbm)
+        )[i]
+        part = pl.ds(pl.multiple_of(c * (PER * LANES), PER * LANES), PER * LANES)
+        return pltpu.make_async_copy(
+            source.at[:, :, part], target.at[:, :, part], out_sem.at[i, c]
+        )
+
+    small[0].start()
+    for c in range(CHUNKS):
+        incopy(0, c).start()
+        incopy(1, c).start()
+    for c in range(CHUNKS):
+        incopy(2, c).start()
+    small[1].start()
+    for c in range(CHUNKS):
+        incopy(3, c).start()
+
     barrier = pltpu.get_barrier_semaphore()
     for d in range(1, n_ctx):
         pl.semaphore_signal(barrier, inc=1, device_id={"ctx": lax.rem(me + d, n_ctx)})
     for d in range(1, n_dp):
         pl.semaphore_signal(barrier, inc=1, device_id={"dp": lax.rem(mydp + d, n_dp)})
 
+    small[0].wait()
     docs = lengths_ref.shape[1]
     offset = me * T
     first, last = jnp.int32(1 << 20), jnp.int32(-(1 << 20))
@@ -118,31 +153,54 @@
             device_id={"ctx": lax.rem(me - d + n_ctx, n_ctx)},
         )
 
-    def loop(lo, hi, body):
-        def step(p, _):
-            body(p)
+    def each(f, *lists):
+        return [f(*items) for items in zip(*lists)]
+
+    def chunk_loop(body):
+        def step(c, _):
+            body(c)
             return 0
-        lax.fori_loop(lo, hi, step, 0)
-
-    def state_of(p):
-        own[p] = compact(tn(k_ref[0, :, lanes(p)] * masks[3], v_ref[0, :, lanes(p)]))
-
-    for c in range(CHUNKS):
-        loop(c * PER, (c + 1) * PER, state_of)
-        if c == 0:
+        lax.fori_loop(0, CHUNKS, step, 0)
+
+    def groups(c, size):
+        return [[c * PER + g + i for i in range(size)] for g in range(0, PER, size)]
+
+    def states(c):
+        incopy(0, c).wait()
+        incopy(1, c).wait()
+        for ps in groups(c, 4):
+            ks = [k_ref[0, :, lanes(p)] * masks[3] for p in ps]
+            full = [tn(k, v_ref[0, :, lanes(p)]) for k, p in zip(ks, ps)]
+            for p, x in zip(ps, full):
+                own[p] = compact(x)
+
+        @pl.when(c == 0)
+        def _():
             pl.semaphore_wait(barrier, n_ctx + n_dp - 2)
+
         for d in range(1, reach + 1):
             @pl.when(me + d < n_ctx)
             def _():
                 fcopy(d, c).start()
 
-    def inside(p):
-        q, k, v = q_ref[0, :, lanes(p)], k_ref[0, :, lanes(p)], v_ref[0, :, lanes(p)]
-        w = nt(stack(q), k).astype(BF) * doc_mask[...]
-        weights[p] = w
-        att_s[p] = nn(jnp.concatenate([w[:T], w[T:]], axis=1), stack(v))
-
-    loop(0, PAIRS, inside)
+    chunk_loop(states)
+
+    def inside(c):
+        incopy(2, c).wait()
+        for ps in groups(c, 2):
+            qs = [stack(q_ref[0, :, lanes(p)]) for p in ps]
+            scores = [nt(q, k_ref[0, :, lanes(p)]) for q, p in zip(qs, ps)]
+            ws = [x.astype(BF) * doc_mask[...] for x in scores]
+            for p, w in zip(ps, ws):
+                weights[p] = w
+            atts = [
+                nn(jnp.concatenate([w[:T], w[T:]], axis=1), stack(v_ref[0, :, lanes(p)]))
+                for w, p in zip(ws, ps)
+            ]
+            for p, att in zip(ps, atts):
+                att_s[p] = att
+
+    chunk_loop(inside)
 
     jrow = lax.broadcasted_iota(jnp.int32, (2 * LANES, LANES), 0)
     jlane = lax.broadcasted_iota(jnp.int32, (2 * LANES, LANES), 1)
@@ -153,35 +211,53 @@
         low = (x - high.astype(F32)).astype(BF)
         return nn(jnp.concatenate([high, low], axis=1), mean_of)
 
-    def normalize(p):
-        c = fbuf[0, p].astype(F32) * coef_f[1]
+    def gather(buf, coef, p):
+        c = buf[0, p].astype(F32) * coef[1]
         for d in range(2, reach + 1):
-            c += fbuf[d - 1, p].astype(F32) * coef_f[d]
-        c = c.astype(BF)
-        carried[p] = c
-        qb = q_ref[0, :, lanes(p)] * masks[2]
-        att = att_s[p] + nn(qb, diag(c))
-        inv = lax.rsqrt(head_mean(att * att) + EPS)
-        normed = att * inv
-        gain = gain_ref[:, lanes(p)]
-        out_ref[0, :, lanes(p)] = (gain * normed).astype(BF)
-        dy = dy_ref[0, :, lanes(p)].astype(F32)
-        dn = dy * gain
-        gatt = ((dn - normed * head_mean(dn * normed)) * inv).astype(BF)
-        gatt_s[p] = gatt
-        gain_ctx[me, pl.ds(p, 1)] = jnp.sum(dy * normed, axis=0, keepdims=True)
-        back[p] = compact(tn(qb, gatt))
-
-    for c in range(CHUNKS):
+            c += buf[d - 1, p].astype(F32) * coef[d]
+        return c.astype(BF)
+
+    small[1].wait()
+
+    def normalize(c):
         for d in range(1, reach + 1):
             @pl.when(me - d >= 0)
             def _():
                 fcopy(d, c).wait_recv()
-        loop(c * PER, (c + 1) * PER, normalize)
+        incopy(3, c).wait()
+        for ps in groups(c, 4):
+            cs = [gather(fbuf, coef_f, p) for p in ps]
+            for p, x in zip(ps, cs):
+                carried[p] = x
+            qbs = [q_ref[0, :, lanes(p)] * masks[2] for p in ps]
+            atts = [att_s[p] + nn(qb, diag(x)) for p, qb, x in zip(ps, qbs, cs)]
+            means = [head_mean(att * att) for att in atts]
+            invs = [lax.rsqrt(m + EPS) for m in means]
+            normeds = each(lambda att, inv: att * inv, atts, invs)
+            gains = [gain_ref[:, lanes(p)] for p in ps]
+            for p, gain, normed in zip(ps, gains, normeds):
+                out_ref[0, :, lanes(p)] = (gain * normed).astype(BF)
+            dys = [dy_ref[0, :, lanes(p)].astype(F32) for p in ps]
+            terms = each(lambda dy, normed: dy * normed, dys, normeds)
+            for p, term in zip(ps, terms):
+                gain_ctx[me, pl.ds(p, 1)] = jnp.sum(term, axis=0, keepdims=True)
+            means = each(lambda term, gain: head_mean(term * gain), terms, gains)
+            gatts = [
+                ((dy * gain - normed * m) * inv).astype(BF)
+                for dy, gain, normed, m, inv in zip(dys, gains, normeds, means, invs)
+            ]
+            for p, gatt in zip(ps, gatts):
+                gatt_s[p] = gatt
+            full = each(tn, qbs, gatts)
+            for p, x in zip(ps, full):
+                back[p] = compact(x)
         for d in range(1, reach + 1):
             @pl.when(me - d >= 0)
             def _():
                 bcopy(d, c).start()
+        outcopy(0, c).start()
+
+    chunk_loop(normalize)
 
     def gcopy(d, slot):
         return pltpu.make_async_remote_copy(
@@ -200,18 +276,26 @@
     for d in range(1, n_ctx):
         gcopy(d, me).start()
 
-    def gradients(p):
-        q, k, v = q_ref[0, :, lanes(p)], k_ref[0, :, lanes(p)], v_ref[0, :, lanes(p)]
-        gatt = gatt_s[p]
-        gs = stack(gatt)
-        gw = nt(gs, v).astype(BF) * doc_mask[...]
-        gq = nn(jnp.concatenate([gw[:T], gw[T:]], axis=1), stack(k))
-        gq += nt(gatt * masks[2], diag(carried[p]))
-        gq_ref[0, :, lanes(p)] = gq.astype(BF)
-        gk_s[p] = tn(gw, stack(q))
-        gv_s[p] = tn(weights[p], gs)
-
-    loop(0, PAIRS, gradients)
+    def gradients(c):
+        for ps in groups(c, 2):
+            gatts = [gatt_s[p] for p in ps]
+            gss = each(stack, gatts)
+            scores = [nt(gs, v_ref[0, :, lanes(p)]) for gs, p in zip(gss, ps)]
+            for p, gs in zip(ps, gss):
+                gv_s[p] = tn(weights[p], gs)
+            gws = [x.astype(BF) * doc_mask[...] for x in scores]
+            gqs = [
+                nn(jnp.concatenate([gw[:T], gw[T:]], axis=1), stack(k_ref[0, :, lanes(p)]))
+                + nt(gatt * masks[2], diag(carried[p]))
+                for gw, gatt, p in zip(gws, gatts, ps)
+            ]
+            for p, gq in zip(ps, gqs):
+                gq_ref[0, :, lanes(p)] = gq.astype(BF)
+            for p, gw in zip(ps, gws):
+                gk_s[p] = tn(gw, stack(q_ref[0, :, lanes(p)]))
+        outcopy(1, c).start()
+
+    chunk_loop(gradients)
 
     for d in range(1, n_ctx):
         gcopy(d, lax.rem(me - d + n_ctx, n_ctx)).wait_recv()
@@ -222,21 +306,23 @@
     for d in range(1, n_dp):
         hcopy(d, mydp).start()
 
-    def finish(p):
-        c = bbuf[0, p].astype(F32) * coef_b[1]
-        for d in range(2, reach + 1):
-            c += bbuf[d - 1, p].astype(F32) * coef_b[d]
-        bd = diag(c.astype(BF))
-        after = masks[3]
-        gk_ref[0, :, lanes(p)] = (gk_s[p] + nt(v_ref[0, :, lanes(p)] * after, bd)).astype(BF)
-        gv_ref[0, :, lanes(p)] = (gv_s[p] + nn(k_ref[0, :, lanes(p)] * after, bd)).astype(BF)
-
-    for c in range(CHUNKS):
+    def finish(c):
         for d in range(1, reach + 1):
             @pl.when(me + d < n_ctx)
             def _():
                 bcopy(d, c).wait_recv()
-        loop(c * PER, (c + 1) * PER, finish)
+        for ps in groups(c, 4):
+            bds = [diag(gather(bbuf, coef_b, p)) for p in ps]
+            after = masks[3]
+            gks = [nt(v_ref[0, :, lanes(p)] * after, bd) for p, bd in zip(ps, bds)]
+            gvs = [nn(k_ref[0, :, lanes(p)] * after, bd) for p, bd in zip(ps, bds)]
+            for p, gk, gv in zip(ps, gks, gvs):
+                gk_ref[0, :, lanes(p)] = (gk_s[p] + gk).astype(BF)
+                gv_ref[0, :, lanes(p)] = (gv_s[p] + gv).astype(BF)
+        outcopy(2, c).start()
+        outcopy(3, c).start()
+
+    chunk_loop(finish)
 
     for d in range(1, n_dp):
         hcopy(d, lax.rem(mydp - d + n_dp, n_dp)).wait_recv()
@@ -244,6 +330,8 @@
     for i in range(1, n_dp):
         total += gain_dp[i]
     gg_ref[...] = total * (1.0 / math.sqrt(total_tokens))
+    gg_copy = pltpu.make_async_copy(gg_ref, gg_hbm, gg_sem)
+    gg_copy.start()
 
     for c in range(CHUNKS):
         for d in range(1, reach + 1):
@@ -258,6 +346,22 @@
         gcopy(d, me).wait_send()
     for d in range(1, n_dp):
         hcopy(d, mydp).wait_send()
+    for i in range(4):
+        for c in range(CHUNKS):
+            outcopy(i, c).wait()
+    gg_copy.wait()
+
+
+def write_out(*refs):
+    sources, targets, sems = refs[:5], refs[5:10], refs[10]
+    copies = [
+        pltpu.make_async_copy(source, target, sems.at[i])
+        for i, (source, target) in enumerate(zip(sources, targets))
+    ]
+    for copy in copies:
+        copy.start()
+    for copy in copies:
+        copy.wait()
 
 
 def per_device(queries, keys, values, grad_output, out_gain, doc_lengths):
@@ -266,15 +370,31 @@
     length = T * n_ctx
     longest = length // 3
     reach = min(n_ctx - 1, -(-(longest - 1) // T))
-    vmem = pl.BlockSpec(memory_space=pltpu.VMEM)
+    hbm = pl.BlockSpec(memory_space=pltpu.HBM)
     data = jax.ShapeDtypeStruct((1, T, width), BF)
     dma = pltpu.SemaphoreType.DMA
+    shapes = (data,) * 4 + (jax.ShapeDtypeStruct((PAIRS, LANES), F32),)
     out = pl.pallas_call(
         functools.partial(kernel, n_ctx, n_dp, reach, n_dp * length),
-        out_shape=(data,) * 4 + (jax.ShapeDtypeStruct((PAIRS, LANES), F32),),
-        in_specs=[pl.BlockSpec(memory_space=pltpu.SMEM)] + [vmem] * 5,
-        out_specs=(vmem,) * 5,
+        out_shape=shapes,
+        in_specs=[hbm] * 6,
+        out_specs=(hbm,) * 5,
         scratch_shapes=[
+            pltpu.SMEM(doc_lengths.shape, jnp.int32),
+            pltpu.VMEM((1, T, width), BF),
+            pltpu.VMEM((1, T, width), BF),
+            pltpu.VMEM((1, T, width), BF),
+            pltpu.VMEM((1, T, width), BF),
+            pltpu.VMEM((1, width), F32),
+            dma((4, CHUNKS)),
+            dma((2,)),
+            pltpu.VMEM((1, T, width), BF),
+            pltpu.VMEM((1, T, width), BF),
+            pltpu.VMEM((1, T, width), BF),
+            pltpu.VMEM((1, T, width), BF),
+            pltpu.VMEM((PAIRS, LANES), F32),
+            dma((4, CHUNKS)),
+            dma,
             pltpu.VMEM((4, T, LANES), BF),
             pltpu.VMEM((2 * T, T), BF),
             pltpu.VMEM((PAIRS, E, LANES), BF),
@@ -295,9 +415,17 @@
             dma((n_dp - 1,)), dma((n_dp - 1,)),
         ],
         compiler_params=pltpu.CompilerParams(
-            collective_id=0, has_side_effects=True, vmem_limit_bytes=48 * 1024 * 1024
+            collective_id=0, has_side_effects=True, vmem_limit_bytes=VMEM_LIMIT
         ),
     )(doc_lengths, queries, keys, values, grad_output, out_gain.reshape(1, width))
+    out = pl.pallas_call(
+        write_out,
+        out_shape=shapes,
+        in_specs=[hbm] * 5,
+        out_specs=(hbm,) * 5,
+        scratch_shapes=[dma((5,))],
+        compiler_params=pltpu.CompilerParams(vmem_limit_bytes=VMEM_LIMIT),
+    )(*out)
     return (*out[:4], out[4].reshape(width))
 
 

time: 48.3 us -> 101 us (2.09)
  the two profiles are of different devices: /device:TPU:4 before, /device:TPU:0 now
where the time goes in v2:
time: 101 us
  Pallas kernels  100 us (99%)
    pallas_call x1, Pallas kernels, per_device(): pl.pallas_call(write_out, out_shape=shapes, in_specs=[hbm] * 5, out_specs...  64.9 us
    pallas_call x1, Pallas kernels, per_device(): pl.pallas_call(functools.partial(kernel, n_ctx, n_dp, reach, n_dp * lengt...  35.4 us

profile of v2, /device:TPU:0, one launch (start us, length us, event | category | flops | bytes accessed | tf_op | source)
XLA Modules:
  0.0 101.0 jit_solution(9768003876370866522)
XLA Ops:
  0.6 35.4 %shard_map.101 = (bf16[1,128,2048]{2,1,0:T(8,128)(2,1)}, bf16[1,128,2048]{2,1,0:T(8,128)(2,1)}, bf16[1,128,2048]{2,1,0:T(8,128)(2,1)}, bf16[1,128,2048]{2,1,0:T(8,128)(2,1)}, f32[16,128]{1,0:T(8,128)}) custom-call(s32[1,12]{1,0:T(1,128)} %lengths_hbm.1, bf16[1,128,2048]{2,1,0:T(8,128)(2,1)} %q_hbm.1, bf16[1,128,2048]{2,1,0:T(8,128)(2,1)} %k_hbm.1, ...), custom_call_target="tpu_custom_call" | custom-call | tf_op jit(solution)/shard_map/pallas_call | solution.py:377
  36.0 64.9 %shard_map.102 = (bf16[1,128,2048]{2,1,0:T(8,128)(2,1)}, bf16[1,128,2048]{2,1,0:T(8,128)(2,1)}, bf16[1,128,2048]{2,1,0:T(8,128)(2,1)}, bf16[1,128,2048]{2,1,0:T(8,128)(2,1)}, f32[16,128]{1,0:T(8,128)}) custom-call(bf16[1,128,2048]{2,1,0:T(8,128)(2,1)} %get-tuple-element.15.refs_0_, bf16[1,128,2048]{2,1,0:T(8,128)(2,1)} %get-tuple-element.16.refs_1_, ...), custom_call_target="tpu_custom_call" | custom-call | tf_op jit(solution)/shard_map/pallas_call | solution.py:421

commit v3 on v2

--- a/solution.py
+++ b/solution.py
@@ -14,6 +14,7 @@
 PAIRS = H // 2
 CHUNKS = 4
 PER = PAIRS // CHUNKS
+HALF = PER // 2
 EPS = 1e-05
 VMEM_LIMIT = 58 * 1024 * 1024
 BF = jnp.bfloat16
@@ -38,11 +39,14 @@
     out_hbm, gq_hbm, gk_hbm, gv_hbm, gg_hbm,
     lengths_ref, q_ref, k_ref, v_ref, dy_ref, gain_ref, in_sem, small_sem,
     out_ref, gq_ref, gk_ref, gv_ref, gg_ref, out_sem, gg_sem,
-    masks, doc_mask, own, back, fbuf, bbuf, carried, weights, att_s, gatt_s, gk_s, gv_s,
+    masks, doc_mask, own, back, fnear, bnear, fsum, bsum, fbuf, bbuf, fenter, benter, carried, weights, att_s, gatt_s, gk_s, gv_s,
     gain_ctx, gain_dp,
-    fsend, frecv, bsend, brecv, gsend, grecv, hsend, hrecv,
+    fsems, bsems, gsend, grecv, hsend, hrecv,
 ):
     me = lax.axis_index("ctx")
+    chip, side = me // 2, lax.rem(me, 2)
+    partner = me + 1 - 2 * side
+    n_chips = n_ctx // 2
     mydp = lax.axis_index("dp")
     T = q_ref.shape[1]
 
@@ -87,6 +91,7 @@
     docs = lengths_ref.shape[1]
     offset = me * T
     first, last = jnp.int32(1 << 20), jnp.int32(-(1 << 20))
+    hits_even, hits_odd = jnp.int32(0), jnp.int32(0)
     hits_f = [jnp.int32(0)] * (reach + 1)
     hits_b = [jnp.int32(0)] * (reach + 1)
     row = lax.broadcasted_iota(jnp.int32, (T, T), 0)
@@ -97,14 +102,24 @@
     for i in range(docs):
         first = jnp.where(begin >= 0, jnp.minimum(first, begin), first)
         last = jnp.where(begin < T, jnp.maximum(last, begin), last)
+        base = begin + side * T
         for d in range(2, reach + 1):
-            hits_f[d] += jnp.where((begin >= -(d - 1) * T) & (begin < 0), 1, 0)
-            hits_b[d] += jnp.where((begin >= T) & (begin < d * T), 1, 0)
+            hits_f[d] += jnp.where((base >= -(d - 1) * 2 * T) & (base < 0), 1, 0)
+            hits_b[d] += jnp.where((base >= 2 * T) & (base < d * 2 * T), 1, 0)
+        hits_even += jnp.where((base >= 0) & (base < T), 1, 0)
+        hits_odd += jnp.where((base >= T) & (base < 2 * T), 1, 0)
         id_row += (row >= begin).astype(jnp.int32)
         id_col += (col >= begin).astype(jnp.int32)
         begin = begin + lengths_ref[0, i]
     coef_f = [jnp.where(hits_f[d] == 0, 1.0, 0.0).astype(F32) for d in range(reach + 1)]
     coef_b = [jnp.where(hits_b[d] == 0, 1.0, 0.0).astype(F32) for d in range(reach + 1)]
+    keep_even = jnp.where(hits_even == 0, 1.0, 0.0).astype(F32)
+    keep_odd = jnp.where(hits_odd == 0, 1.0, 0.0).astype(F32)
+    odd = jnp.where(side == 1, 1.0, 0.0).astype(F32)
+    sum_f = (odd + (1.0 - odd) * keep_odd, (1.0 - odd) + odd * keep_odd)
+    sum_b = ((1.0 - odd) + odd * keep_even, odd + (1.0 - odd) * keep_even)
+    enter_f = (odd, (1.0 - odd) + odd * keep_even)
+    enter_b = (1.0 - odd, odd + (1.0 - odd) * keep_odd)
     dm = jnp.where((row >= col) & (id_row == id_col), 1.0, 0.0).astype(BF)
     doc_mask[0:T] = dm
     doc_mask[T:2 * T] = dm
@@ -116,11 +131,11 @@
     masks[3] = jnp.where(trow >= last, 1.0, 0.0).astype(BF)
 
     for d in range(1, reach + 1):
-        @pl.when(me - d < 0)
+        @pl.when(chip - d < 0)
         def _():
             fbuf[d - 1] = jnp.zeros(fbuf.shape[1:], BF)
 
-        @pl.when(me + d >= n_ctx)
+        @pl.when(chip + d >= n_chips)
         def _():
             bbuf[d - 1] = jnp.zeros(bbuf.shape[1:], BF)
 
@@ -137,30 +152,94 @@
     def stack(x):
         return jnp.concatenate([x * masks[0], x * masks[1]], axis=0)
 
-    def fcopy(d, c):
-        part = pl.ds(c * PER, PER)
-        return pltpu.make_async_remote_copy(
-            src_ref=own.at[part], dst_ref=fbuf.at[d - 1, part],
-            send_sem=fsend.at[d - 1, c], recv_sem=frecv.at[d - 1, c],
-            device_id={"ctx": lax.rem(me + d, n_ctx)},
-        )
-
-    def bcopy(d, c):
-        part = pl.ds(c * PER, PER)
-        return pltpu.make_async_remote_copy(
-            src_ref=back.at[part], dst_ref=bbuf.at[d - 1, part],
-            send_sem=bsend.at[d - 1, c], recv_sem=brecv.at[d - 1, c],
-            device_id={"ctx": lax.rem(me - d + n_ctx, n_ctx)},
-        )
+    def whole(c):
+        return pl.ds(c * PER, PER)
+
+    def mine(c):
+        return pl.ds(c * PER + side * HALF, HALF)
+
+    def links(state, near, summed, buf, enter, sems, sign):
+        send, recv, far_send, far_recv, last_send, last_recv = sems
+
+        def first_hop(c):
+            return pltpu.make_async_remote_copy(
+                src_ref=state.at[whole(c)], dst_ref=near.at[whole(c)],
+                send_sem=send.at[c], recv_sem=recv.at[c], device_id={"ctx": partner},
+            )
+
+        def far_hop(d, c):
+            return pltpu.make_async_remote_copy(
+                src_ref=summed.at[mine(c)], dst_ref=buf.at[d - 1, mine(c)],
+                send_sem=far_send.at[d - 1, c], recv_sem=far_recv.at[d - 1, c],
+                device_id={"ctx": lax.rem(me + sign * 2 * d + n_ctx, n_ctx)},
+            )
+
+        def last_hop(c):
+            return pltpu.make_async_remote_copy(
+                src_ref=enter.at[mine(c)], dst_ref=enter.at[mine(c)],
+                send_sem=last_send.at[c], recv_sem=last_recv.at[c],
+                device_id={"ctx": partner},
+            )
+
+        def other_last_hop(c):
+            theirs = pl.ds(c * PER + (1 - side) * HALF, HALF)
+            return pltpu.make_async_remote_copy(
+                src_ref=enter.at[theirs], dst_ref=enter.at[theirs],
+                send_sem=last_send.at[c], recv_sem=last_recv.at[c],
+                device_id={"ctx": partner},
+            )
+
+        def sends(d):
+            return chip + d < n_chips if sign > 0 else chip - d >= 0
+
+        def gets(d):
+            return chip - d >= 0 if sign > 0 else chip + d < n_chips
+
+        return first_hop, far_hop, last_hop, other_last_hop, sends, gets
+
+    forward = links(own, fnear, fsum, fbuf, fenter, fsems, 1)
+    backward = links(back, bnear, bsum, bbuf, benter, bsems, -1)
+
+    def combine(c, link, state, near, summed, take):
+        first_hop, far_hop, _, _, sends, _ = link
+        first_hop(c).wait_recv()
+        x = state[mine(c)].astype(F32) * take[0] + near[mine(c)].astype(F32) * take[1]
+        summed[mine(c)] = x.astype(BF)
+        for d in range(1, reach + 1):
+            @pl.when(sends(d))
+            def _():
+                far_hop(d, c).start()
+
+    def relay(c, link, buf, enter, coef):
+        _, far_hop, last_hop, _, _, gets = link
+        for d in range(1, reach + 1):
+            @pl.when(gets(d))
+            def _():
+                far_hop(d, c).wait_recv()
+        x = buf[0, mine(c)].astype(F32) * coef[1]
+        for d in range(2, reach + 1):
+            x += buf[d - 1, mine(c)].astype(F32) * coef[d]
+        enter[mine(c)] = x.astype(BF)
+        last_hop(c).start()
+
+    def drain(link):
+        first_hop, far_hop, last_hop, _, sends, _ = link
+        for c in range(CHUNKS):
+            first_hop(c).wait_send()
+            last_hop(c).wait_send()
+            for d in range(1, reach + 1):
+                @pl.when(sends(d))
+                def _():
+                    far_hop(d, c).wait_send()
 
     def each(f, *lists):
         return [f(*items) for items in zip(*lists)]
 
-    def chunk_loop(body):
+    def chunk_loop(body, low=0, high=CHUNKS):
         def step(c, _):
             body(c)
             return 0
-        lax.fori_loop(0, CHUNKS, step, 0)
+        lax.fori_loop(low, high, step, 0)
 
     def groups(c, size):
         return [[c * PER + g + i for i in range(size)] for g in range(0, PER, size)]
@@ -178,12 +257,10 @@
         def _():
             pl.semaphore_wait(barrier, n_ctx + n_dp - 2)
 
-        for d in range(1, reach + 1):
-            @pl.when(me + d < n_ctx)
-            def _():
-                fcopy(d, c).start()
+        forward[0](c).start()
 
     chunk_loop(states)
+    chunk_loop(lambda c: combine(c, forward, own, fnear, fsum, sum_f))
 
     def inside(c):
         incopy(2, c).wait()
@@ -200,7 +277,13 @@
             for p, att in zip(ps, atts):
                 att_s[p] = att
 
-    chunk_loop(inside)
+    def inside_and_relay(c):
+        inside(c)
+        for i in range(2):
+            relay(2 * c - CHUNKS + i, forward, fbuf, fenter, coef_f)
+
+    chunk_loop(inside, 0, CHUNKS // 2)
+    chunk_loop(inside_and_relay, CHUNKS // 2)
 
     jrow = lax.broadcasted_iota(jnp.int32, (2 * LANES, LANES), 0)
     jlane = lax.broadcasted_iota(jnp.int32, (2 * LANES, LANES), 1)
@@ -211,22 +294,16 @@
         low = (x - high.astype(F32)).astype(BF)
         return nn(jnp.concatenate([high, low], axis=1), mean_of)
 
-    def gather(buf, coef, p):
-        c = buf[0, p].astype(F32) * coef[1]
-        for d in range(2, reach + 1):
-            c += buf[d - 1, p].astype(F32) * coef[d]
-        return c.astype(BF)
+    def gather(near, enter, take, p):
+        return (near[p].astype(F32) * take[0] + enter[p].astype(F32) * take[1]).astype(BF)
 
     small[1].wait()
 
     def normalize(c):
-        for d in range(1, reach + 1):
-            @pl.when(me - d >= 0)
-            def _():
-                fcopy(d, c).wait_recv()
+        forward[3](c).wait_recv()
         incopy(3, c).wait()
         for ps in groups(c, 4):
-            cs = [gather(fbuf, coef_f, p) for p in ps]
+            cs = [gather(fnear, fenter, enter_f, p) for p in ps]
             for p, x in zip(ps, cs):
                 carried[p] = x
             qbs = [q_ref[0, :, lanes(p)] * masks[2] for p in ps]
@@ -251,13 +328,11 @@
             full = each(tn, qbs, gatts)
             for p, x in zip(ps, full):
                 back[p] = compact(x)
-        for d in range(1, reach + 1):
-            @pl.when(me - d >= 0)
-            def _():
-                bcopy(d, c).start()
+        backward[0](c).start()
         outcopy(0, c).start()
 
     chunk_loop(normalize)
+    chunk_loop(lambda c: combine(c, backward, back, bnear, bsum, sum_b))
 
     def gcopy(d, slot):
         return pltpu.make_async_remote_copy(
@@ -295,7 +370,13 @@
                 gk_s[p] = tn(gw, stack(q_ref[0, :, lanes(p)]))
         outcopy(1, c).start()
 
-    chunk_loop(gradients)
+    def gradients_and_relay(c):
+        gradients(c)
+        for i in range(2):
+            relay(2 * c - CHUNKS + i, backward, bbuf, benter, coef_b)
+
+    chunk_loop(gradients, 0, CHUNKS // 2)
+    chunk_loop(gradients_and_relay, CHUNKS // 2)
 
     for d in range(1, n_ctx):
         gcopy(d, lax.rem(me - d + n_ctx, n_ctx)).wait_recv()
@@ -307,12 +388,9 @@
         hcopy(d, mydp).start()
 
     def finish(c):
-        for d in range(1, reach + 1):
-            @pl.when(me + d < n_ctx)
-            def _():
-                bcopy(d, c).wait_recv()
+        backward[3](c).wait_recv()
         for ps in groups(c, 4):
-            bds = [diag(gather(bbuf, coef_b, p)) for p in ps]
+            bds = [diag(gather(bnear, benter, enter_b, p)) for p in ps]
             after = masks[3]
             gks = [nt(v_ref[0, :, lanes(p)] * after, bd) for p, bd in zip(ps, bds)]
             gvs = [nn(k_ref[0, :, lanes(p)] * after, bd) for p, bd in zip(ps, bds)]
@@ -333,15 +411,8 @@
     gg_copy = pltpu.make_async_copy(gg_ref, gg_hbm, gg_sem)
     gg_copy.start()
 
-    for c in range(CHUNKS):
-        for d in range(1, reach + 1):
-            @pl.when(me + d < n_ctx)
-            def _():
-                fcopy(d, c).wait_send()
-
-            @pl.when(me - d >= 0)
-            def _():
-                bcopy(d, c).wait_send()
+    drain(forward)
+    drain(backward)
     for d in range(1, n_ctx):
         gcopy(d, me).wait_send()
     for d in range(1, n_dp):
@@ -353,15 +424,30 @@
 
 
 def write_out(*refs):
-    sources, targets, sems = refs[:5], refs[5:10], refs[10]
-    copies = [
-        pltpu.make_async_copy(source, target, sems.at[i])
-        for i, (source, target) in enumerate(zip(sources, targets))
-    ]
-    for copy in copies:
-        copy.start()
-    for copy in copies:
-        copy.wait()
+    sources, targets, held, in_sems, out_sems = refs[:5], refs[5:10], refs[10:15], refs[15], refs[16]
+
+    def copies(from_refs, to_refs, sems):
+        made = []
+        for i, (source, target) in enumerate(zip(from_refs, to_refs)):
+            if i == 4:
+                made.append(pltpu.make_async_copy(source, target, sems.at[i, 0]))
+                continue
+            rows = source.shape[1] // 2
+            for h in range(2):
+                part = pl.ds(h * rows, rows)
+                made.append(
+                    pltpu.make_async_copy(source.at[:, part], target.at[:, part], sems.at[i, h])
+                )
+        return made
+
+    loads, stores = copies(sources, held, in_sems), copies(held, targets, out_sems)
+    for load in loads:
+        load.start()
+    for load, store in zip(loads, stores):
+        load.wait()
+        store.start()
+    for store in stores:
+        store.wait()
 
 
 def per_device(queries, keys, values, grad_output, out_gain, doc_lengths):
@@ -369,10 +455,13 @@
     n_ctx, n_dp = lax.axis_size("ctx"), lax.axis_size("dp")
     length = T * n_ctx
     longest = length // 3
-    reach = min(n_ctx - 1, -(-(longest - 1) // T))
+    reach = min(n_ctx // 2 - 1, -(-(longest - 1) // (2 * T)))
+    state = pltpu.VMEM((PAIRS, E, LANES), BF)
+    far = pltpu.VMEM((reach, PAIRS, E, LANES), BF)
     hbm = pl.BlockSpec(memory_space=pltpu.HBM)
     data = jax.ShapeDtypeStruct((1, T, width), BF)
     dma = pltpu.SemaphoreType.DMA
+    hops = [dma((CHUNKS,))] * 2 + [dma((reach, CHUNKS))] * 2 + [dma((CHUNKS,))] * 2
     shapes = (data,) * 4 + (jax.ShapeDtypeStruct((PAIRS, LANES), F32),)
     out = pl.pallas_call(
         functools.partial(kernel, n_ctx, n_dp, reach, n_dp * length),
@@ -397,11 +486,8 @@
             dma,
             pltpu.VMEM((4, T, LANES), BF),
             pltpu.VMEM((2 * T, T), BF),
-            pltpu.VMEM((PAIRS, E, LANES), BF),
-            pltpu.VMEM((PAIRS, E, LANES), BF),
-            pltpu.VMEM((reach, PAIRS, E, LANES), BF),
-            pltpu.VMEM((reach, PAIRS, E, LANES), BF),
-            pltpu.VMEM((PAIRS, E, LANES), BF),
+            state, state, state, state, state, state,
+            far, far, state, state, state,
             pltpu.VMEM((PAIRS, 2 * T, T), BF),
             pltpu.VMEM((PAIRS, T, LANES), F32),
             pltpu.VMEM((PAIRS, T, LANES), BF),
@@ -409,8 +495,7 @@
             pltpu.VMEM((PAIRS, T, LANES), F32),
             pltpu.VMEM((n_ctx, PAIRS, LANES), F32),
             pltpu.VMEM((n_dp, PAIRS, LANES), F32),
-            dma((reach, CHUNKS)), dma((reach, CHUNKS)),
-            dma((reach, CHUNKS)), dma((reach, CHUNKS)),
+            hops, hops,
             dma((n_ctx - 1,)), dma((n_ctx - 1,)),
             dma((n_dp - 1,)), dma((n_dp - 1,)),
         ],
@@ -423,7 +508,8 @@
         out_shape=shapes,
         in_specs=[hbm] * 5,
         out_specs=(hbm,) * 5,
-        scratch_shapes=[dma((5,))],
+        scratch_shapes=[pltpu.VMEM(x.shape, x.dtype) for x in shapes]
+        + [dma((5, 2)), dma((5, 2))],
         compiler_params=pltpu.CompilerParams(vmem_limit_bytes=VMEM_LIMIT),
     )(*out)
     return (*out[:4], out[4].reshape(width))

time: 101 us -> 30.7 us (0.30)
  Pallas kernels: 100 us -> 29.9 us
    pallas_call x1, Pallas kernels: 64.9 us -> 2.43 us  [per_device(): pl.pallas_call(write_out, out_shape=shapes, in_specs=[hbm] * 5, out_specs...]
    pallas_call x1, Pallas kernels: 35.4 us -> 27.5 us  [per_device(): pl.pallas_call(functools.partial(kernel, n_ctx, n_dp, reach, n_dp * lengt...]
where the time goes in v3:
time: 30.7 us; the launch traced here: 30.6 us
  Pallas kernels  29.9 us (97%)
  between operations  0.64 us (2%)
    pallas_call x1, Pallas kernels, per_device(): pl.pallas_call(functools.partial(kernel, n_ctx, n_dp, reach, n_dp * lengt...  27.5 us
    pallas_call x1, Pallas kernels, per_device(): pl.pallas_call(write_out, out_shape=shapes, in_specs=[hbm] * 5, out_specs...  2.43 us

profile of v3, /device:TPU:0, one launch (start us, length us, event | category | flops | bytes accessed | tf_op | source)
XLA Modules:
  0.0 30.6 jit_solution(14517126772798874998)
XLA Ops:
  0.6 27.5 %shard_map.101 = (bf16[1,128,2048]{2,1,0:T(8,128)(2,1)}, bf16[1,128,2048]{2,1,0:T(8,128)(2,1)}, bf16[1,128,2048]{2,1,0:T(8,128)(2,1)}, bf16[1,128,2048]{2,1,0:T(8,128)(2,1)}, f32[16,128]{1,0:T(8,128)}) custom-call(s32[1,12]{1,0:T(1,128)} %lengths_hbm.1, bf16[1,128,2048]{2,1,0:T(8,128)(2,1)} %q_hbm.1, bf16[1,128,2048]{2,1,0:T(8,128)(2,1)} %k_hbm.1, ...), custom_call_target="tpu_custom_call" | custom-call | tf_op jit(solution)/shard_map/pallas_call | solution.py:466
  28.1 2.4 %shard_map.102 = (bf16[1,128,2048]{2,1,0:T(8,128)(2,1)}, bf16[1,128,2048]{2,1,0:T(8,128)(2,1)}, bf16[1,128,2048]{2,1,0:T(8,128)(2,1)}, bf16[1,128,2048]{2,1,0:T(8,128)(2,1)}, f32[16,128]{1,0:T(8,128)}) custom-call(bf16[1,128,2048]{2,1,0:T(8,128)(2,1)} %get-tuple-element.15.refs_0_, bf16[1,128,2048]{2,1,0:T(8,128)(2,1)} %get-tuple-element.16.refs_1_, ...), custom_call_target="tpu_custom_call" | custom-call | tf_op jit(solution)/shard_map/pallas_call | solution.py:506

commit v4 on v3

--- a/solution.py
+++ b/solution.py
@@ -222,6 +222,27 @@
         enter[mine(c)] = x.astype(BF)
         last_hop(c).start()
 
+    def combine_forward(c):
+        combine(c, forward, own, fnear, fsum, sum_f)
+
+    def combine_backward(c):
+        combine(c, backward, back, bnear, bsum, sum_b)
+
+    def relay_forward(c):
+        relay(c, forward, fbuf, fenter, coef_f)
+
+    def relay_backward(c):
+        relay(c, backward, bbuf, benter, coef_b)
+
+    def exchange(c, combine_one, relay_one):
+        @pl.when(c == 0)
+        def _():
+            combine_one(CHUNKS - 1)
+
+        @pl.when(c > 0)
+        def _():
+            relay_one(c - 1)
+
     def drain(link):
         first_hop, far_hop, last_hop, _, sends, _ = link
         for c in range(CHUNKS):
@@ -259,8 +280,11 @@
 
         forward[0](c).start()
 
+        @pl.when(c > 0)
+        def _():
+            combine_forward(c - 1)
+
     chunk_loop(states)
-    chunk_loop(lambda c: combine(c, forward, own, fnear, fsum, sum_f))
 
     def inside(c):
         incopy(2, c).wait()
@@ -276,23 +300,21 @@
             ]
             for p, att in zip(ps, atts):
                 att_s[p] = att
-
-    def inside_and_relay(c):
-        inside(c)
-        for i in range(2):
-            relay(2 * c - CHUNKS + i, forward, fbuf, fenter, coef_f)
-
-    chunk_loop(inside, 0, CHUNKS // 2)
-    chunk_loop(inside_and_relay, CHUNKS // 2)
+        exchange(c, combine_forward, relay_forward)
+
+    chunk_loop(inside)
+    relay_forward(CHUNKS - 1)
 
     jrow = lax.broadcasted_iota(jnp.int32, (2 * LANES, LANES), 0)
     jlane = lax.broadcasted_iota(jnp.int32, (2 * LANES, LANES), 1)
     mean_of = jnp.where((lax.rem(jrow, LANES) < E) == (jlane < E), 1.0 / E, 0.0).astype(BF)
 
-    def head_mean(x):
+    def head_means(xs):
+        x = jnp.concatenate(xs, axis=0)
         high = x.astype(BF)
         low = (x - high.astype(F32)).astype(BF)
-        return nn(jnp.concatenate([high, low], axis=1), mean_of)
+        means = nn(jnp.concatenate([high, low], axis=1), mean_of)
+        return [means[i * T:(i + 1) * T] for i in range(len(xs))]
 
     def gather(near, enter, take, p):
         return (near[p].astype(F32) * take[0] + enter[p].astype(F32) * take[1]).astype(BF)
@@ -308,7 +330,7 @@
                 carried[p] = x
             qbs = [q_ref[0, :, lanes(p)] * masks[2] for p in ps]
             atts = [att_s[p] + nn(qb, diag(x)) for p, qb, x in zip(ps, qbs, cs)]
-            means = [head_mean(att * att) for att in atts]
+            means = head_means([att * att for att in atts])
             invs = [lax.rsqrt(m + EPS) for m in means]
             normeds = each(lambda att, inv: att * inv, atts, invs)
             gains = [gain_ref[:, lanes(p)] for p in ps]
@@ -318,7 +340,7 @@
             terms = each(lambda dy, normed: dy * normed, dys, normeds)
             for p, term in zip(ps, terms):
                 gain_ctx[me, pl.ds(p, 1)] = jnp.sum(term, axis=0, keepdims=True)
-            means = each(lambda term, gain: head_mean(term * gain), terms, gains)
+            means = head_means(each(lambda term, gain: term * gain, terms, gains))
             gatts = [
                 ((dy * gain - normed * m) * inv).astype(BF)
                 for dy, gain, normed, m, inv in zip(dys, gains, normeds, means, invs)
@@ -331,8 +353,11 @@
         backward[0](c).start()
         outcopy(0, c).start()
 
+        @pl.when(c > 0)
+        def _():
+            combine_backward(c - 1)
+
     chunk_loop(normalize)
-    chunk_loop(lambda c: combine(c, backward, back, bnear, bsum, sum_b))
 
     def gcopy(d, slot):
         return pltpu.make_async_remote_copy(
@@ -369,14 +394,10 @@
             for p, gw in zip(ps, gws):
                 gk_s[p] = tn(gw, stack(q_ref[0, :, lanes(p)]))
         outcopy(1, c).start()
-
-    def gradients_and_relay(c):
-        gradients(c)
-        for i in range(2):
-            relay(2 * c - CHUNKS + i, backward, bbuf, benter, coef_b)
-
-    chunk_loop(gradients, 0, CHUNKS // 2)
-    chunk_loop(gradients_and_relay, CHUNKS // 2)
+        exchange(c, combine_backward, relay_backward)
+
+    chunk_loop(gradients)
+    relay_backward(CHUNKS - 1)
 
     for d in range(1, n_ctx):
         gcopy(d, lax.rem(me - d + n_ctx, n_ctx)).wait_recv()

time: 30.7 us -> 30 us (0.977)
  Pallas kernels: 29.9 us -> 29.2 us
    pallas_call x1, Pallas kernels: 27.5 us -> 26.8 us  [per_device(): pl.pallas_call(functools.partial(kernel, n_ctx, n_dp, reach, n_dp * lengt...]
where the time goes in v4:
time: 30 us; the launch traced here: 29.9 us
  Pallas kernels  29.2 us (97%)
  between operations  0.64 us (2%)
    pallas_call x1, Pallas kernels, per_device(): pl.pallas_call(functools.partial(kernel, n_ctx, n_dp, reach, n_dp * lengt...  26.8 us
    pallas_call x1, Pallas kernels, per_device(): pl.pallas_call(write_out, out_shape=shapes, in_specs=[hbm] * 5, out_specs...  2.43 us

profile of v4, /device:TPU:0, one launch (start us, length us, event | category | flops | bytes accessed | tf_op | source)
XLA Modules:
  0.0 29.9 jit_solution(13628982736522955654)
XLA Ops:
  0.6 26.8 %shard_map.101 = (bf16[1,128,2048]{2,1,0:T(8,128)(2,1)}, bf16[1,128,2048]{2,1,0:T(8,128)(2,1)}, bf16[1,128,2048]{2,1,0:T(8,128)(2,1)}, bf16[1,128,2048]{2,1,0:T(8,128)(2,1)}, f32[16,128]{1,0:T(8,128)}) custom-call(s32[1,12]{1,0:T(1,128)} %lengths_hbm.1, bf16[1,128,2048]{2,1,0:T(8,128)(2,1)} %q_hbm.1, bf16[1,128,2048]{2,1,0:T(8,128)(2,1)} %k_hbm.1, ...), custom_call_target="tpu_custom_call" | custom-call | tf_op jit(solution)/shard_map/pallas_call | solution.py:487
  27.4 2.4 %shard_map.102 = (bf16[1,128,2048]{2,1,0:T(8,128)(2,1)}, bf16[1,128,2048]{2,1,0:T(8,128)(2,1)}, bf16[1,128,2048]{2,1,0:T(8,128)(2,1)}, bf16[1,128,2048]{2,1,0:T(8,128)(2,1)}, f32[16,128]{1,0:T(8,128)}) custom-call(bf16[1,128,2048]{2,1,0:T(8,128)(2,1)} %get-tuple-element.15.refs_0_, bf16[1,128,2048]{2,1,0:T(8,128)(2,1)} %get-tuple-element.16.refs_1_, ...), custom_call_target="tpu_custom_call" | custom-call | tf_op jit(solution)/shard_map/pallas_call | solution.py:527

commit v5 on v4

--- a/solution.py
+++ b/solution.py
@@ -288,7 +288,7 @@
 
     def inside(c):
         incopy(2, c).wait()
-        for ps in groups(c, 2):
+        for ps in groups(c, 4):
             qs = [stack(q_ref[0, :, lanes(p)]) for p in ps]
             scores = [nt(q, k_ref[0, :, lanes(p)]) for q, p in zip(qs, ps)]
             ws = [x.astype(BF) * doc_mask[...] for x in scores]
@@ -377,7 +377,7 @@
         gcopy(d, me).start()
 
     def gradients(c):
-        for ps in groups(c, 2):
+        for ps in groups(c, 4):
             gatts = [gatt_s[p] for p in ps]
             gss = each(stack, gatts)
             scores = [nt(gs, v_ref[0, :, lanes(p)]) for gs, p in zip(gss, ps)]

time: 30 us -> 30 us (level)
  no operation moved by 1% of the time
where the time goes in v5:
time: 30 us; the launch traced here: 29.9 us
  Pallas kernels  29.2 us (97%)
  between operations  0.64 us (2%)
    pallas_call x1, Pallas kernels, per_device(): pl.pallas_call(functools.partial(kernel, n_ctx, n_dp, reach, n_dp * lengt...  26.8 us
    pallas_call x1, Pallas kernels, per_device(): pl.pallas_call(write_out, out_shape=shapes, in_specs=[hbm] * 5, out_specs...  2.43 us

profile of v5, /device:TPU:0, one launch (start us, length us, event | category | flops | bytes accessed | tf_op | source)
XLA Modules:
  0.0 29.9 jit_solution(9467357367063845428)
XLA Ops:
  0.6 26.8 %shard_map.101 = (bf16[1,128,2048]{2,1,0:T(8,128)(2,1)}, bf16[1,128,2048]{2,1,0:T(8,128)(2,1)}, bf16[1,128,2048]{2,1,0:T(8,128)(2,1)}, bf16[1,128,2048]{2,1,0:T(8,128)(2,1)}, f32[16,128]{1,0:T(8,128)}) custom-call(s32[1,12]{1,0:T(1,128)} %lengths_hbm.1, bf16[1,128,2048]{2,1,0:T(8,128)(2,1)} %q_hbm.1, bf16[1,128,2048]{2,1,0:T(8,128)(2,1)} %k_hbm.1, ...), custom_call_target="tpu_custom_call" | custom-call | tf_op jit(solution)/shard_map/pallas_call | solution.py:487
  27.4 2.4 %shard_map.102 = (bf16[1,128,2048]{2,1,0:T(8,128)(2,1)}, bf16[1,128,2048]{2,1,0:T(8,128)(2,1)}, bf16[1,128,2048]{2,1,0:T(8,128)(2,1)}, bf16[1,128,2048]{2,1,0:T(8,128)(2,1)}, f32[16,128]{1,0:T(8,128)}) custom-call(bf16[1,128,2048]{2,1,0:T(8,128)(2,1)} %get-tuple-element.15.refs_0_, bf16[1,128,2048]{2,1,0:T(8,128)(2,1)} %get-tuple-element.16.refs_1_, ...), custom_call_target="tpu_custom_call" | custom-call | tf_op jit(solution)/shard_map/pallas_call | solution.py:527

commit v6 on v5

--- a/solution.py
+++ b/solution.py
@@ -41,7 +41,7 @@
     out_ref, gq_ref, gk_ref, gv_ref, gg_ref, out_sem, gg_sem,
     masks, doc_mask, own, back, fnear, bnear, fsum, bsum, fbuf, bbuf, fenter, benter, carried, weights, att_s, gatt_s, gk_s, gv_s,
     gain_ctx, gain_dp,
-    fsems, bsems, gsend, grecv, hsend, hrecv,
+    fsems, bsems, gsend, grecv, hsend, hrecv, csend, crecv,
 ):
     me = lax.axis_index("ctx")
     chip, side = me // 2, lax.rem(me, 2)
@@ -84,8 +84,14 @@
     barrier = pltpu.get_barrier_semaphore()
     for d in range(1, n_ctx):
         pl.semaphore_signal(barrier, inc=1, device_id={"ctx": lax.rem(me + d, n_ctx)})
-    for d in range(1, n_dp):
-        pl.semaphore_signal(barrier, inc=1, device_id={"dp": lax.rem(mydp + d, n_dp)})
+
+    hub = n_ctx - 1
+
+    @pl.when(me == hub)
+    def _():
+        for d in range(1, n_dp):
+            pl.semaphore_signal(barrier, inc=1, device_id={"dp": lax.rem(mydp + d, n_dp)})
+
 
     small[0].wait()
     docs = lengths_ref.shape[1]
@@ -276,7 +282,13 @@
 
         @pl.when(c == 0)
         def _():
-            pl.semaphore_wait(barrier, n_ctx + n_dp - 2)
+            @pl.when(me == hub)
+            def _():
+                pl.semaphore_wait(barrier, n_ctx + n_dp - 2)
+
+            @pl.when(me != hub)
+            def _():
+                pl.semaphore_wait(barrier, n_ctx - 1)
 
         forward[0](c).start()
 
@@ -359,11 +371,16 @@
 
     chunk_loop(normalize)
 
-    def gcopy(d, slot):
+    def gcopy(slot):
         return pltpu.make_async_remote_copy(
             src_ref=gain_ctx.at[slot], dst_ref=gain_ctx.at[slot],
-            send_sem=gsend.at[d - 1], recv_sem=grecv.at[d - 1],
-            device_id={"ctx": lax.rem(me + d, n_ctx)},
+            send_sem=gsend, recv_sem=grecv.at[slot], device_id={"ctx": hub},
+        )
+
+    def ccopy(i):
+        return pltpu.make_async_remote_copy(
+            src_ref=gg_ref, dst_ref=gg_ref,
+            send_sem=csend.at[i], recv_sem=crecv, device_id={"ctx": i},
         )
 
     def hcopy(d, slot):
@@ -373,10 +390,35 @@
             device_id={"dp": lax.rem(mydp + d, n_dp)},
         )
 
-    for d in range(1, n_ctx):
-        gcopy(d, me).start()
+    @pl.when(me != hub)
+    def _():
+        gcopy(me).start()
+
+    def sum_sequence():
+        for i in range(n_ctx - 1):
+            gcopy(i).wait_recv()
+        total = gain_ctx[0]
+        for i in range(1, n_ctx):
+            total += gain_ctx[i]
+        gain_dp[mydp] = total
+        for d in range(1, n_dp):
+            hcopy(d, mydp).start()
+
+    def sum_all():
+        for d in range(1, n_dp):
+            hcopy(d, lax.rem(mydp - d + n_dp, n_dp)).wait_recv()
+        total = gain_dp[0]
+        for i in range(1, n_dp):
+            total += gain_dp[i]
+        gg_ref[...] = total * (1.0 / math.sqrt(total_tokens))
+        for i in range(n_ctx - 1):
+            ccopy(i).start()
 
     def gradients(c):
+        @pl.when((me == hub) & (c == CHUNKS // 2))
+        def _():
+            sum_sequence()
+
         for ps in groups(c, 4):
             gatts = [gatt_s[p] for p in ps]
             gss = each(stack, gatts)
@@ -399,16 +441,11 @@
     chunk_loop(gradients)
     relay_backward(CHUNKS - 1)
 
-    for d in range(1, n_ctx):
-        gcopy(d, lax.rem(me - d + n_ctx, n_ctx)).wait_recv()
-    total = gain_ctx[0]
-    for i in range(1, n_ctx):
-        total += gain_ctx[i]
-    gain_dp[mydp] = total
-    for d in range(1, n_dp):
-        hcopy(d, mydp).start()
-
     def finish(c):
+        @pl.when((me == hub) & (c == CHUNKS - 1))
+        def _():
+            sum_all()
+
         backward[3](c).wait_recv()
         for ps in groups(c, 4):
             bds = [diag(gather(bnear, benter, enter_b, p)) for p in ps]
@@ -423,21 +460,26 @@
 
     chunk_loop(finish)
 
-    for d in range(1, n_dp):
-        hcopy(d, lax.rem(mydp - d + n_dp, n_dp)).wait_recv()
-    total = gain_dp[0]
-    for i in range(1, n_dp):
-        total += gain_dp[i]
-    gg_ref[...] = total * (1.0 / math.sqrt(total_tokens))
+    @pl.when(me != hub)
+    def _():
+        ccopy(0).wait_recv()
+
     gg_copy = pltpu.make_async_copy(gg_ref, gg_hbm, gg_sem)
     gg_copy.start()
 
     drain(forward)
     drain(backward)
-    for d in range(1, n_ctx):
-        gcopy(d, me).wait_send()
-    for d in range(1, n_dp):
-        hcopy(d, mydp).wait_send()
+    @pl.when(me != hub)
+    def _():
+        gcopy(me).wait_send()
+
+    @pl.when(me == hub)
+    def _():
+        for d in range(1, n_dp):
+            hcopy(d, mydp).wait_send()
+        for i in range(n_ctx - 1):
+            ccopy(i).wait_send()
+
     for i in range(4):
         for c in range(CHUNKS):
             outcopy(i, c).wait()
@@ -517,8 +559,9 @@
             pltpu.VMEM((n_ctx, PAIRS, LANES), F32),
             pltpu.VMEM((n_dp, PAIRS, LANES), F32),
             hops, hops,
-            dma((n_ctx - 1,)), dma((n_ctx - 1,)),
+            dma, dma((n_ctx - 1,)),
             dma((n_dp - 1,)), dma((n_dp - 1,)),
+            dma((n_ctx - 1,)), dma,
         ],
         compiler_params=pltpu.CompilerParams(
             collective_id=0, has_side_effects=True, vmem_limit_bytes=VMEM_LIMIT

time: 30 us -> 30.9 us (1.030)
  Pallas kernels: 29.2 us -> 30.1 us
    pallas_call x1, Pallas kernels: 26.8 us -> 27.7 us  [per_device(): pl.pallas_call(functools.partial(kernel, n_ctx, n_dp, reach, n_dp * lengt...]
where the time goes in v6:
time: 30.9 us; the launch traced here: 30.8 us
  Pallas kernels  30.1 us (97%)
  between operations  0.64 us (2%)
    pallas_call x1, Pallas kernels, per_device(): pl.pallas_call(functools.partial(kernel, n_ctx, n_dp, reach, n_dp * lengt...  27.7 us
    pallas_call x1, Pallas kernels, per_device(): pl.pallas_call(write_out, out_shape=shapes, in_specs=[hbm] * 5, out_specs...  2.43 us

profile of v6, /device:TPU:0, one launch (start us, length us, event | category | flops | bytes accessed | tf_op | source)
XLA Modules:
  0.0 30.8 jit_solution(8880388472052766069)
XLA Ops:
  0.6 27.7 %shard_map.101 = (bf16[1,128,2048]{2,1,0:T(8,128)(2,1)}, bf16[1,128,2048]{2,1,0:T(8,128)(2,1)}, bf16[1,128,2048]{2,1,0:T(8,128)(2,1)}, bf16[1,128,2048]{2,1,0:T(8,128)(2,1)}, f32[16,128]{1,0:T(8,128)}) custom-call(s32[1,12]{1,0:T(1,128)} %lengths_hbm.1, bf16[1,128,2048]{2,1,0:T(8,128)(2,1)} %q_hbm.1, bf16[1,128,2048]{2,1,0:T(8,128)(2,1)} %k_hbm.1, ...), custom_call_target="tpu_custom_call" | custom-call | tf_op jit(solution)/shard_map/pallas_call | solution.py:529
  28.3 2.4 %shard_map.102 = (bf16[1,128,2048]{2,1,0:T(8,128)(2,1)}, bf16[1,128,2048]{2,1,0:T(8,128)(2,1)}, bf16[1,128,2048]{2,1,0:T(8,128)(2,1)}, bf16[1,128,2048]{2,1,0:T(8,128)(2,1)}, f32[16,128]{1,0:T(8,128)}) custom-call(bf16[1,128,2048]{2,1,0:T(8,128)(2,1)} %get-tuple-element.15.refs_0_, bf16[1,128,2048]{2,1,0:T(8,128)(2,1)} %get-tuple-element.16.refs_1_, ...), custom_call_target="tpu_custom_call" | custom-call | tf_op jit(solution)/shard_map/pallas_call | solution.py:570

commit v7 on v5

--- a/solution.py
+++ b/solution.py
@@ -376,6 +376,16 @@
     for d in range(1, n_ctx):
         gcopy(d, me).start()
 
+    def sum_sequence():
+        for d in range(1, n_ctx):
+            gcopy(d, lax.rem(me - d + n_ctx, n_ctx)).wait_recv()
+        total = gain_ctx[0]
+        for i in range(1, n_ctx):
+            total += gain_ctx[i]
+        gain_dp[mydp] = total
+        for d in range(1, n_dp):
+            hcopy(d, mydp).start()
+
     def gradients(c):
         for ps in groups(c, 4):
             gatts = [gatt_s[p] for p in ps]
@@ -396,17 +406,12 @@
         outcopy(1, c).start()
         exchange(c, combine_backward, relay_backward)
 
+        @pl.when(c == CHUNKS - 2)
+        def _():
+            sum_sequence()
+
     chunk_loop(gradients)
     relay_backward(CHUNKS - 1)
-
-    for d in range(1, n_ctx):
-        gcopy(d, lax.rem(me - d + n_ctx, n_ctx)).wait_recv()
-    total = gain_ctx[0]
-    for i in range(1, n_ctx):
-        total += gain_ctx[i]
-    gain_dp[mydp] = total
-    for d in range(1, n_dp):
-        hcopy(d, mydp).start()
 
     def finish(c):
         backward[3](c).wait_recv()

time: 30 us -> 29.6 us (0.987)
  Pallas kernels: 29.2 us -> 28.8 us
    pallas_call x1, Pallas kernels: 26.8 us -> 26.3 us  [per_device(): pl.pallas_call(functools.partial(kernel, n_ctx, n_dp, reach, n_dp * lengt...]
where the time goes in v7:
time: 29.6 us; the launch traced here: 29.4 us
  Pallas kernels  28.8 us (97%)
  between operations  0.64 us (2%)
    pallas_call x1, Pallas kernels, per_device(): pl.pallas_call(functools.partial(kernel, n_ctx, n_dp, reach, n_dp * lengt...  26.3 us
    pallas_call x1, Pallas kernels, per_device(): pl.pallas_call(write_out, out_shape=shapes, in_specs=[hbm] * 5, out_specs...  2.43 us

profile of v7, /device:TPU:0, one launch (start us, length us, event | category | flops | bytes accessed | tf_op | source)
XLA Modules:
  0.0 29.4 jit_solution(9223855629518902248)
XLA Ops:
  0.6 26.3 %shard_map.101 = (bf16[1,128,2048]{2,1,0:T(8,128)(2,1)}, bf16[1,128,2048]{2,1,0:T(8,128)(2,1)}, bf16[1,128,2048]{2,1,0:T(8,128)(2,1)}, bf16[1,128,2048]{2,1,0:T(8,128)(2,1)}, f32[16,128]{1,0:T(8,128)}) custom-call(s32[1,12]{1,0:T(1,128)} %lengths_hbm.1, bf16[1,128,2048]{2,1,0:T(8,128)(2,1)} %q_hbm.1, bf16[1,128,2048]{2,1,0:T(8,128)(2,1)} %k_hbm.1, ...), custom_call_target="tpu_custom_call" | custom-call | tf_op jit(solution)/shard_map/pallas_call | solution.py:492
  27.0 2.4 %shard_map.102 = (bf16[1,128,2048]{2,1,0:T(8,128)(2,1)}, bf16[1,128,2048]{2,1,0:T(8,128)(2,1)}, bf16[1,128,2048]{2,1,0:T(8,128)(2,1)}, bf16[1,128,2048]{2,1,0:T(8,128)(2,1)}, f32[16,128]{1,0:T(8,128)}) custom-call(bf16[1,128,2048]{2,1,0:T(8,128)(2,1)} %get-tuple-element.15.refs_0_, bf16[1,128,2048]{2,1,0:T(8,128)(2,1)} %get-tuple-element.16.refs_1_, ...), custom_call_target="tpu_custom_call" | custom-call | tf_op jit(solution)/shard_map/pallas_call | solution.py:532
